TPU v7x, 256 devices: a whole 4x4x8 slice. The times are simulated.
256 devices in a mesh: slide: 8 (over z), tile: 32 (over y, x, core).
Axes of the slice: x: 4, y: 4, z: 8, core: 2. Of those that a mesh axis runs over, the one named last changes fastest.
Arguments:
- features: bfloat16 [8, 448, 98, 384], P('slide', 'tile'), may hold values from -6 to 6
- cotangent: bfloat16 [8, 448, 98, 384], P('slide', 'tile'), may hold values from -6 to 6
- owner_slot: int32 [8, 64, 14], P('slide'), may hold values from -1 to 511, as said below
- dw_weight: float32 [7, 7, 384], replicated, may hold values from -0.875 to 0.875
- dw_bias: float32 [384], replicated, may hold values from -3 to 3
- ln_gain: float32 [384], replicated, may hold values from 0.1 to 1.9
- ln_bias: float32 [384], replicated, may hold values from -3 to 3
- w_in: bfloat16 [384, 1536], replicated, may hold values from -0.3125 to 0.3125
- b_in: float32 [1536], replicated, may hold values from -3 to 3
- w_out: bfloat16 [1536, 384], replicated, may hold values from -0.15625 to 0.15625
- b_out: float32 [384], replicated, may hold values from -3 to 3
- layer_scale: float32 [384], replicated, may hold values from 0.25 to 1
Outputs:
- mixed: bfloat16 [8, 448, 98, 384], P('slide', 'tile')
- grad_dw_weight: float32 [7, 7, 384], replicated
- grad_dw_bias: float32 [384], replicated
- grad_ln_gain: float32 [384], replicated
- grad_ln_bias: float32 [384], replicated
- grad_w_in: float32 [384, 1536], replicated
- grad_b_in: float32 [1536], replicated
- grad_w_out: float32 [1536, 384], replicated
- grad_b_out: float32 [384], replicated
- grad_layer_scale: float32 [384], replicated
Inputs may be any that keep to these rules, and one draw needn't show every extreme that they name: `owner_slot`: -1 marks a background tile; every other value o names owner device o // 16; each value 0 to 511 appears exactly once in each slide, so every owner device holds 16 tissue tiles. Of the tissue tiles in the 2 rows of one device, at most 1 goes to any one owner device, and for some pair of sender and owner exactly 1 does. In each slide the 2 rows of one device are tissue in all 14 columns.
All inputs are finite; a program needn't handle non-finite values.
Results may differ from a plain program's by a relative error of at most 0.0071.
Values may be sent and summed in bfloat16 or wider, within the bound.
A program may use at most 128 MiB of HBM per device.

v0:
```python
import math

import jax
import jax.numpy as jnp
from jax import lax
from jax.experimental import pallas as pl
from jax.experimental.pallas import tpu as pltpu
from jax.sharding import PartitionSpec as P

C = 384
HID = 1536
K = 7
TP = 7
COLS = 14
OWN = 16
ROWS = 14
BREADTH = 98
WIDE = 104
CELLS = ROWS * WIDE
PADDED = 1536
REACH = 3
CHUNK = 512
CHUNKS = HID // CHUNK
PAIR = 2 * WIDE
GROUPS = C // 128
LOSS_SCALE = 1.0 / math.sqrt(8 * 32 * OWN * TP * TP)

CORES = 2
SIZES = {"x": 4, "y": 4, "z": 8}
LANES = 128
MESH = pl.DeviceIdType.MESH


def coordinates():
    tile = lax.axis_index("tile")
    return {
        "z": lax.axis_index("slide"),
        "y": tile // 8,
        "x": (tile // 2) % 4,
        "core": tile % 2,
    }


def device_at(where):
    return (where["z"], where["y"] * 8 + where["x"] * 2 + where["core"])


def peer_along(where, axis, distance):
    size = SIZES[axis]
    position = (where[axis] + distance) % size
    return position, device_at({**where, axis: position})


def enter(where):
    tile = lax.axis_index("tile")
    peers = [device_at({**where, "core": 1 - where["core"]})]
    peers += [(where["z"], (tile + step) % 32) for step in (1, 31)]
    for axis, size in SIZES.items():
        peers += [peer_along(where, axis, step)[1] for step in range(1, size)]
    barrier = pltpu.get_barrier_semaphore()
    for peer in peers:
        pl.semaphore_signal(barrier, inc=1, device_id=peer, device_id_type=MESH)
    pl.semaphore_wait(barrier, len(peers))


class Sum:
    def __init__(self, rows, dtype, scatter, exchange):
        self.rows, self.dtype = rows, dtype
        self.scatter, self.exchange = scatter, exchange
        self.heights = [rows]
        for axis in scatter:
            self.heights.append(self.heights[-1] // SIZES[axis])
        self.copies = 2 + 2 * sum(SIZES[a] - 1 for a in scatter) + sum(SIZES[a] - 1 for a in exchange)

    def scratch(self):
        shapes = [pltpu.VMEM((self.rows, LANES), jnp.float32)]
        for axis, before, after in zip(self.scatter, self.heights, self.heights[1:]):
            shapes.append(pltpu.VMEM((before, LANES), jnp.float32))
            shapes.append(pltpu.VMEM((before, LANES), self.dtype))
            shapes.append(pltpu.VMEM((SIZES[axis] - 1, after, LANES), self.dtype))
        for axis in self.exchange:
            shapes.append(pltpu.VMEM((SIZES[axis], self.heights[-1], LANES), self.dtype))
        shapes.append(pltpu.SemaphoreType.DMA((self.copies,)))
        shapes.append(pltpu.SemaphoreType.DMA((self.copies,)))
        return shapes

    def bind(self, where, keep, send, result, refs):
        refs = list(refs)
        self.where, self.keep, self.send, self.result = where, keep, send, result
        self.landed = refs.pop(0)
        self.levels = [tuple(refs.pop(0) for _ in range(3)) for _ in self.scatter]
        self.slots = [refs.pop(0) for _ in self.exchange]
        self.send_sems, self.recv_sems = refs
        self.used = 0
        self.flying = []
        self.done = []
        self.phase = 0
        offset = 0
        self.offsets = [offset]
        for axis, height in zip(self.scatter, self.heights[1:]):
            offset = offset + where[axis] * height
            self.offsets.append(offset)
        return self

    def copy(self, source, target, device):
        made = pltpu.make_async_remote_copy(
            src_ref=source,
            dst_ref=target,
            send_sem=self.send_sems.at[self.used],
            recv_sem=self.recv_sems.at[self.used],
            device_id=device,
            device_id_type=MESH,
        )
        self.used += 1
        made.start()
        self.flying.append(made)

    def land(self):
        for made in self.flying:
            made.wait_recv()
        self.done += self.flying
        self.flying = []

    def rows_at(self, level):
        return pl.ds(pl.multiple_of(self.offsets[level], 16), self.heights[level])

    def start_core(self):
        other = device_at({**self.where, "core": 1 - self.where["core"]})
        self.copy(self.send, self.landed, other)

    def start_scatter(self, index, total):
        axis, height = self.scatter[index], self.heights[index + 1]
        held, outgoing, incoming = self.levels[index]
        held[...] = total
        outgoing[...] = total.astype(self.dtype)
        for step in range(1, SIZES[axis]):
            position, device = peer_along(self.where, axis, step)
            self.copy(
                outgoing.at[pl.ds(pl.multiple_of(position * height, 16), height), :],
                incoming.at[step - 1],
                device,
            )

    def finish_scatter(self, index):
        axis, height = self.scatter[index], self.heights[index + 1]
        held, _, incoming = self.levels[index]
        total = held[pl.ds(pl.multiple_of(self.where[axis] * height, 16), height), :]
        for step in range(SIZES[axis] - 1):
            total = total + incoming[step].astype(jnp.float32)
        return total

    def start_exchange(self, index, total):
        axis, slots = self.exchange[index], self.slots[index]
        me = self.where[axis]
        slots[me] = total.astype(self.dtype)
        for step in range(1, SIZES[axis]):
            _, device = peer_along(self.where, axis, step)
            self.copy(slots.at[me], slots.at[me], device)

    def finish_exchange(self, index):
        axis, slots = self.exchange[index], self.slots[index]
        total = slots[0].astype(jnp.float32)
        for place in range(1, SIZES[axis]):
            total = total + slots[place].astype(jnp.float32)
        return total

    def start_gather(self, index):
        axis, core = self.scatter[index], self.where["core"]
        block = self.result.at[core, self.rows_at(index + 1), :]
        for step in range(1, SIZES[axis]):
            _, device = peer_along(self.where, axis, step)
            self.copy(block, block, device)

    def advance(self):
        phase, core = self.phase, self.where["core"]
        deep, wide = len(self.scatter), len(self.exchange)
        if phase > 2 * deep + wide + 2:
            return False
        self.phase += 1
        self.land()
        if phase == 0:
            self.start_core()
            return True
        if phase == 1:
            total = self.keep[...] + self.landed[...]
            self.start_scatter(0, total)
            return True
        if phase <= deep + wide:
            if phase <= deep:
                total = self.finish_scatter(phase - 2)
                self.start_scatter(phase - 1, total)
                return True
            index = phase - deep - 1
            total = self.finish_scatter(deep - 1) if index == 0 else self.finish_exchange(index - 1)
            self.start_exchange(index, total)
            return True
        step = phase - deep - wide - 1
        if step == 0:
            total = self.finish_exchange(wide - 1)
            self.result[core, self.rows_at(deep), :] = total.astype(self.dtype)
        if step < deep:
            self.start_gather(deep - 1 - step)
            return True
        if step == deep:
            other = device_at({**self.where, "core": 1 - core})
            self.copy(self.result.at[core], self.result.at[core], other)
            return True
        for made in self.done:
            made.wait_send()
        return False


def lanes(group):
    return slice(group * LANES, (group + 1) * LANES)


def by_eight(value):
    return jnp.sum(value.reshape(-1, 8, LANES), axis=0)


def gelu_parts(pre_act):
    density = jnp.exp(-0.5 * pre_act * pre_act) * 0.3989422804014327
    t = pl.reciprocal(1.0 + 0.2316419 * jnp.abs(pre_act), approx=False)
    series = 1.781477937 + t * (-1.821255978 + t * 1.330274429)
    series = t * (0.319381530 + t * (-0.356563782 + t * series))
    tail = density * series
    mass = jnp.where(pre_act >= 0.0, 1.0 - tail, tail)
    return pre_act * mass, mass + pre_act * density


def fill(feat, cot, mask, padded, cot_masked):
    edge = jnp.zeros((3, ROWS + 2 * REACH, 8, LANES), jnp.float32)
    padded[:, :, 0:8, :] = edge
    padded[:, :, 104:112, :] = edge
    padded[:, :, 112:120, :] = edge
    cot_masked[:, :, 96:104, :] = jnp.zeros((3, ROWS, 8, LANES), jnp.float32)

    def row(i, carry):
        live = mask[1 + i // TP][:BREADTH]
        cells = feat[i].astype(jnp.float32)
        pull = cot[i].astype(jnp.float32)
        for group in range(GROUPS):
            padded[group, i + REACH, 8 : 8 + BREADTH, :] = cells[:, lanes(group)] * live
            cot_masked[group, i, 0:BREADTH, :] = pull[:, lanes(group)] * live
        return carry

    lax.fori_loop(0, ROWS, row, 0)


def fill_halo(halo, mask, padded):
    def row(i, carry):
        for side in range(2):
            live = mask[3 * side][:BREADTH]
            cells = halo[side, i].astype(jnp.float32)
            for group in range(GROUPS):
                padded[group, i + side * (ROWS + REACH), 8 : 8 + BREADTH, :] = (
                    cells[:, lanes(group)] * live
                )
        return carry

    lax.fori_loop(0, REACH, row, 0)


def spread_taps(weight, taps):
    for tap in range(K * K):
        for group in range(GROUPS):
            taps[group, tap] = jnp.broadcast_to(weight[tap : tap + 1, lanes(group)], (8, LANES))


def conv(padded, taps, bias, conv_out):
    def tile(step, carry):
        group, column = step // 13, step % 13
        total = jnp.zeros((ROWS, 8, LANES), jnp.float32) + bias[group]
        for col_tap in range(K):
            window = padded[group, :, pl.ds(8 * column + 5 + col_tap, 8), :]
            for row_tap in range(K):
                total = total + window[row_tap : row_tap + ROWS] * taps[group, row_tap * K + col_tap]
        conv_out[group, :, pl.ds(pl.multiple_of(8 * column, 8), 8), :] = total
        return carry

    lax.fori_loop(0, GROUPS * 13, tile, 0)


def conv_grad(first, last, padded, grad_conv, tap_sums):
    def tile(step, carry):
        group, column = step // 13, step % 13
        pull = grad_conv[group, :, pl.ds(pl.multiple_of(8 * column, 8), 8), :]
        for col_tap in range(K):
            window = padded[group, :, pl.ds(8 * column + 5 + col_tap, 8), :]
            for row_tap in range(K):
                tap = row_tap * K + col_tap
                tap_sums[group, tap] += jnp.sum(window[row_tap : row_tap + ROWS] * pull, axis=0)
        return carry

    lax.fori_loop(first, last, tile, 0)


def norm(conv_out, inv_std, gain, offset, normed):
    def pair(step, carry):
        rows = pl.ds(2 * step, 2)
        held = [conv_out[group, rows].reshape(PAIR, LANES) for group in range(GROUPS)]
        mean = jnp.sum(held[0] + held[1] + held[2], axis=-1, keepdims=True) * (1.0 / C)
        held = [item - mean for item in held]
        squares = held[0] * held[0] + held[1] * held[1] + held[2] * held[2]
        var = jnp.sum(squares, axis=-1, keepdims=True) * (1.0 / C)
        inv = jnp.broadcast_to(lax.rsqrt(var + 1e-06), (PAIR, LANES))
        inv_std[rows] = inv.reshape(2, WIDE, LANES)
        place = pl.ds(pl.multiple_of(step * PAIR, 16), PAIR)
        for group in range(GROUPS):
            centred = held[group] * inv
            conv_out[group, rows] = centred.reshape(2, WIDE, LANES)
            normed[place, lanes(group)] = (
                centred * gain[:, lanes(group)] + offset[:, lanes(group)]
            ).astype(jnp.bfloat16)
        return carry

    lax.fori_loop(0, ROWS // 2, pair, 0)


def branch_grad(cot_masked, scale, grad_branch, sums):
    def pair(step, carry):
        place = pl.ds(pl.multiple_of(step * PAIR, 16), PAIR)
        for group in range(GROUPS):
            pull = cot_masked[group, pl.ds(2 * step, 2)].reshape(PAIR, LANES)
            pull = pull * (scale[:, lanes(group)] * LOSS_SCALE)
            grad_branch[place, lanes(group)] = pull.astype(jnp.bfloat16)
            sums[group] += by_eight(pull)
        return carry

    lax.fori_loop(0, ROWS // 2, pair, 0)


def turn(rows, turned):
    def block(step, carry):
        place = pl.ds(pl.multiple_of(step * LANES, LANES), LANES)
        turned[:, place] = rows[place, :].T
        return carry

    lax.fori_loop(0, PADDED // LANES, block, 0)


def nt(left, right):
    return lax.dot_general(
        left, right, (((1,), (1,)), ((), ())), preferred_element_type=jnp.float32
    )


def mlp_rows(chunk, first, last, normed, grad_branch, w_in, b_in, w_out, b_out, work):
    hidden, grad_pre, branch, grad_xn, in_sums = work
    units = slice(chunk * CHUNK, (chunk + 1) * CHUNK)

    def block(step, carry):
        place = pl.ds(pl.multiple_of(step * PAIR, 16), PAIR)
        pre_act = jnp.dot(normed[place, :], w_in[:, units], preferred_element_type=jnp.float32)
        pre_act = pre_act + b_in[:, units]
        activ, slope = gelu_parts(pre_act)
        activ = activ.astype(jnp.bfloat16)
        hidden[place, :] = activ
        pull = nt(grad_branch[place, :], w_out[units, :]) * slope
        in_sums[:, units] += jnp.sum(pull.reshape(-1, 8, CHUNK), axis=0)
        pull = pull.astype(jnp.bfloat16)
        grad_pre[place, :] = pull
        out = jnp.dot(activ, w_out[units, :], preferred_element_type=jnp.float32)
        back = nt(pull, w_in[:, units])
        if chunk == 0:
            branch[place, :] = out + b_out[...]
            grad_xn[place, :] = back
        else:
            branch[place, :] += out
            grad_xn[place, :] += back
        return carry

    lax.fori_loop(first, last, block, 0)


def weight_grads(chunk, normed_t, grad_branch_t, hidden, grad_pre, large):
    first = jnp.dot(normed_t[...], grad_pre[...], preferred_element_type=jnp.float32)
    for group in range(CHUNK // LANES):
        large[chunk, 0, group * C : (group + 1) * C, :] = first[:, lanes(group)]
    second = jnp.dot(grad_branch_t[...], hidden[...], preferred_element_type=jnp.float32).T
    for group in range(GROUPS):
        large[chunk, 1, group * CHUNK : (group + 1) * CHUNK, :] = second[:, lanes(group)]


def after_mlp(branch, grad_xn, cot_masked, padded, centred, inv_std, mask, scale, gain, mixed, grad_conv, sums):
    def row(i, carry):
        place = pl.ds(pl.multiple_of(i * WIDE, 8), WIDE)
        live = mask[1 + i // TP]
        inv = inv_std[i]
        pulls, held = [], []
        for group in range(GROUPS):
            out = branch[place, lanes(group)].astype(jnp.bfloat16).astype(jnp.float32)
            sums[3 + group] += by_eight(cot_masked[group, i] * out)
            kept = padded[group, i + REACH, 8 : 8 + WIDE, :] + live * (scale[:, lanes(group)] * out)
            mixed[i, :, lanes(group)] = kept[:BREADTH].astype(jnp.bfloat16)
            pull = grad_xn[place, lanes(group)].astype(jnp.bfloat16).astype(jnp.float32)
            cen = centred[group, i]
            sums[6 + group] += by_eight(pull * cen)
            sums[9 + group] += by_eight(pull)
            pulls.append(pull * gain[:, lanes(group)])
            held.append(cen)
        mean = jnp.sum(pulls[0] + pulls[1] + pulls[2], axis=-1, keepdims=True) * (1.0 / C)
        along = pulls[0] * held[0] + pulls[1] * held[1] + pulls[2] * held[2]
        along = jnp.sum(along, axis=-1, keepdims=True) * (1.0 / C)
        for group in range(GROUPS):
            pull = inv * (pulls[group] - mean - held[group] * along)
            grad_conv[group, i] = pull
            sums[12 + group] += by_eight(pull)
        return carry

    lax.fori_loop(0, ROWS, row, 0)


def collect(tap_sums, sums, in_sums, small):
    def put(place, value):
        small[place // LANES, place % LANES : place % LANES + 1, :] = jnp.sum(
            value, axis=0, keepdims=True
        )

    small[1, 40:LANES, :] = jnp.zeros((LANES - 40, LANES), jnp.float32)
    for group in range(GROUPS):
        for tap in range(K * K):
            put(group * K * K + tap, tap_sums[group, tap])
    for index in range(15):
        value = sums[index]
        put(147 + index, value * LOSS_SCALE if 3 <= index < 6 else value)
    for group in range(HID // LANES):
        put(162 + group, in_sums[:, lanes(group)])


def plan():
    large = [
        Sum(1536, jnp.bfloat16, scatter, exchange)
        for scatter, exchange in ((("x", "z"), ("y",)), (("y", "z"), ("x",)), (("z", "y"), ("x",)))
    ]
    return large + [Sum(128, jnp.float32, ("z",), ("x", "y"))]


def work_scratch():
    def f32(*shape):
        return pltpu.VMEM(shape, jnp.float32)

    def b16(*shape):
        return pltpu.VMEM(shape, jnp.bfloat16)

    return [
        b16(2, REACH, BREADTH, C),
        pltpu.SemaphoreType.DMA((2,)),
        pltpu.SemaphoreType.DMA((2,)),
        f32(GROUPS, ROWS + 2 * REACH, 120, LANES),
        f32(GROUPS, ROWS, WIDE, LANES),
        f32(GROUPS, K * K, 8, LANES),
        f32(GROUPS, ROWS, WIDE, LANES),
        f32(ROWS, WIDE, LANES),
        b16(PADDED, C),
        b16(PADDED, C),
        b16(C, PADDED),
        b16(C, PADDED),
        b16(PADDED, CHUNK),
        b16(PADDED, CHUNK),
        f32(CELLS, C),
        f32(CELLS, C),
        f32(8, HID),
        f32(15, 8, LANES),
        f32(GROUPS, K * K, 8, LANES),
        f32(GROUPS, ROWS, WIDE, LANES),
        f32(CHUNKS, 2, 1536, LANES),
        f32(2, LANES, LANES),
        b16(CHUNKS, 2, 1536, LANES),
        f32(2, LANES, LANES),
        b16(ROWS, BREADTH, C),
        pltpu.SemaphoreType.DMA((3,)),
    ]


def block_kernel(
    feat, cot, mask, dw_weight, dw_bias, gain, offset, w_in, b_in, w_out, b_out, scale,
    mixed_out, large_out, small_out, *refs
):
    refs = list(refs)
    own = len(work_scratch())
    (
        halo, halo_send, halo_recv, padded, cot_masked, taps, centred, inv_std, normed, grad_branch,
        normed_t, grad_branch_t, hidden, grad_pre, branch, grad_xn, in_sums, sums, tap_sums,
        grad_conv, large, small, large_held, small_held, mixed, out_sems,
    ) = refs[:own]
    refs = refs[own:]
    where = coordinates()
    core, tile = where["core"], lax.axis_index("tile")
    enter(where)
    halves = []
    for side, step, first in ((0, 1, ROWS - REACH), (1, 31, 0)):
        made = pltpu.make_async_remote_copy(
            src_ref=feat.at[pl.ds(first, REACH)],
            dst_ref=halo.at[side],
            send_sem=halo_send.at[side],
            recv_sem=halo_recv.at[side],
            device_id=(where["z"], (tile + step) % 32),
            device_id_type=MESH,
        )
        made.start()
        halves.append(made)
    running = []
    for index, item in enumerate(plan()):
        count = len(item.scratch())
        mine, refs = refs[:count], refs[count:]
        if index < CHUNKS:
            keep, send = large.at[index, core], large.at[index, 1 - core]
            item.bind(where, keep, send, large_held.at[index], mine)
        else:
            item.bind(where, small.at[core], small.at[1 - core], small_held, mine)
        running.append(item)

    def advance(*which):
        for index in which:
            running[index].advance()

    fill(feat, cot, mask, padded, cot_masked)
    spread_taps(dw_weight, taps)
    sums[...] = jnp.zeros(sums.shape, jnp.float32)
    tap_sums[...] = jnp.zeros(tap_sums.shape, jnp.float32)
    in_sums[...] = jnp.zeros(in_sums.shape, jnp.float32)
    for rows in (normed, grad_branch, hidden, grad_pre):
        rows[CELLS:, :] = jnp.zeros((PADDED - CELLS, rows.shape[1]), jnp.bfloat16)
    branch_grad(cot_masked, scale, grad_branch, sums)
    turn(grad_branch, grad_branch_t)
    for made in halves:
        made.wait_recv()
    fill_halo(halo, mask, padded)
    conv(padded, taps, dw_bias, centred)
    norm(centred, inv_std, gain, offset, normed)
    turn(normed, normed_t)

    work = (hidden, grad_pre, branch, grad_xn, in_sums)
    weights = (normed, grad_branch, w_in, b_in, w_out, b_out, work)
    between = ((), (0,), (0, 1))
    for chunk in range(CHUNKS):
        mlp_rows(chunk, 0, 4, *weights)
        advance(*between[chunk])
        mlp_rows(chunk, 4, 7, *weights)
        weight_grads(chunk, normed_t, grad_branch_t, hidden, grad_pre, large)
        advance(*range(chunk + 1))
    after_mlp(
        branch, grad_xn, cot_masked, padded, centred, inv_std, mask, scale, gain, mixed, grad_conv, sums
    )
    mixed_copy = pltpu.make_async_copy(mixed, mixed_out, out_sems.at[0])
    mixed_copy.start()
    advance(0, 1, 2)
    steps = (0, 10, 20, 30, 39)
    for first, last in zip(steps, steps[1:]):
        conv_grad(first, last, padded, grad_conv, tap_sums)
        if last < 39:
            advance(0, 1, 2)
    collect(tap_sums, sums, in_sums, small)
    going = [running[3], running[0], running[1], running[2]]
    while going:
        going = [item for item in going if item.advance()]
    copies = [
        pltpu.make_async_copy(large_held, large_out, out_sems.at[1]),
        pltpu.make_async_copy(small_held, small_out, out_sems.at[2]),
    ]
    for made in copies:
        made.start()
    for made in copies + [mixed_copy]:
        made.wait()
    for made in halves:
        made.wait_send()


def run_block(*operands):
    scratch = work_scratch()
    for item in plan():
        scratch += item.scratch()
    return pl.pallas_call(
        block_kernel,
        out_shape=(
            jax.ShapeDtypeStruct((ROWS, BREADTH, C), jnp.bfloat16),
            jax.ShapeDtypeStruct((CHUNKS, 2, 1536, LANES), jnp.bfloat16),
            jax.ShapeDtypeStruct((2, LANES, LANES), jnp.float32),
        ),
        in_specs=[pl.BlockSpec(memory_space=pltpu.VMEM)] * len(operands),
        out_specs=(pl.BlockSpec(memory_space=pl.ANY),) * 3,
        scratch_shapes=scratch,
        compiler_params=pltpu.CompilerParams(
            collective_id=0, has_side_effects=True, vmem_limit_bytes=60 * 1024 * 1024
        ),
    )(*operands)


def finish_kernel(mixed_in, large, small, mixed, dw, dwb, ln_gain, ln_bias, w1, b1, w2, b2, scale):
    mixed[...] = mixed_in[...]
    for chunk in range(CHUNKS):
        for group in range(CHUNK // LANES):
            first = chunk * CHUNK + group * LANES
            w1[:, first : first + LANES] = large[chunk, 0, group * C : (group + 1) * C, :].astype(
                jnp.float32
            )
        for group in range(GROUPS):
            w2[chunk * CHUNK : (chunk + 1) * CHUNK, lanes(group)] = large[
                chunk, 1, group * CHUNK : (group + 1) * CHUNK, :
            ].astype(jnp.float32)

    def row(place):
        return small[place // LANES, place % LANES : place % LANES + 1, :]

    for group in range(GROUPS):
        for tap in range(K * K):
            dw[tap // K, tap % K : tap % K + 1, lanes(group)] = row(group * K * K + tap)
    for index, target in enumerate((b2, scale, ln_gain, ln_bias, dwb)):
        for group in range(GROUPS):
            target[:, lanes(group)] = row(147 + index * GROUPS + group)
    for group in range(HID // LANES):
        b1[:, lanes(group)] = row(162 + group)


def finish(mixed, large, small):
    def f32(*shape):
        return jax.ShapeDtypeStruct(shape, jnp.float32)

    vector = f32(1, C)
    return pl.pallas_call(
        finish_kernel,
        out_shape=(
            jax.ShapeDtypeStruct(mixed.shape, mixed.dtype), f32(K, K, C), vector, vector, vector,
            f32(C, HID), f32(1, HID), f32(HID, C), vector, vector,
        ),
        in_specs=[pl.BlockSpec(memory_space=pltpu.VMEM)] * 3,
        out_specs=(pl.BlockSpec(memory_space=pltpu.VMEM),) * 10,
        compiler_params=pltpu.CompilerParams(vmem_limit_bytes=40 * 1024 * 1024),
    )(mixed, large, small)


def tissue_rows(table):
    live = jnp.pad((table >= 0).astype(jnp.float32), ((1, 1), (0, 0)))
    mine = lax.dynamic_slice_in_dim(live, lax.axis_index("tile") * 2, 4, 0)
    cells = jnp.pad(jnp.repeat(mine, TP, axis=1), ((0, 0), (0, WIDE - BREADTH)))
    return jnp.broadcast_to(cells[:, :, None], (4, WIDE, LANES))


def local(
    features,
    cotangent,
    owner_slot,
    dw_weight,
    dw_bias,
    ln_gain,
    ln_bias,
    w_in,
    b_in,
    w_out,
    b_out,
    layer_scale,
):
    mixed, large, small = run_block(
        features[0],
        cotangent[0],
        tissue_rows(owner_slot[0]),
        dw_weight.reshape(K * K, C),
        dw_bias.reshape(GROUPS, 1, LANES),
        ln_gain.reshape(1, C),
        ln_bias.reshape(1, C),
        w_in,
        b_in.reshape(1, HID),
        w_out,
        b_out.reshape(1, C),
        layer_scale.reshape(1, C),
    )
    mixed, dw, dwb, gain, bias, w1, b1, w2, b2, scale = finish(mixed, large, small)
    return (
        mixed[None],
        dw,
        dwb.reshape(C),
        gain.reshape(C),
        bias.reshape(C),
        w1,
        b1.reshape(HID),
        w2,
        b2.reshape(C),
        scale.reshape(C),
    )


def solution(mesh):
    placed = (
        P("slide", "tile", None, None),
        P("slide", "tile", None, None),
        P("slide", None, None),
        P(),
        P(),
        P(),
        P(),
        P(),
        P(),
        P(),
        P(),
        P(),
    )
    return jax.shard_map(
        local,
        mesh=mesh,
        in_specs=placed,
        out_specs=(P("slide", "tile", None, None), P(), P(), P(), P(), P(), P(), P(), P(), P()),
        check_vma=False,
    )
```

profile of v0, /device:TPU:1, one launch (start us, length us, event | category | flops | bytes accessed | tf_op | source)
XLA Modules:
  0.0 139.6 jit_solution(11157806561248531977)
XLA Ops:
  0.6 1.3 reshape.69.dw_bias
  1.9 1.2 reshape.70.gain
  3.1 1.2 reshape.71.offset
  4.4 1.2 reshape.73.b_out
  5.6 1.2 reshape.74.scale
  6.9 1.3 reshape.72.b_in
  8.2 0.7 broadcast_compare_fusion
  8.9 0.1 dynamic-slice_convert_fusion
  9.0 0.1 copy.23
  9.1 0.1 broadcast_in_dim.12
  9.2 0.1 reshape.67
  9.3 1.5 %reshape.68.dw_weight = f32[49,384]{1,0:T(8,128)} reshape(f32[7,7,384]{2,1,0:T(8,128)} %param.15) | data formatting | bytes 150528 | tf_op jit(solution)/shard_map/reshape | solution.py:658
  10.8 0.8 broadcast_in_dim.13.mask
  11.6 117.6 %shard_map.195 = (bf16[14,98,384]{2,1,0:T(8,128)(2,1)}, bf16[3,2,1536,128]{3,2,1,0:T(8,128)(2,1)}, f32[2,128,128]{2,1,0:T(8,128)}) custom-call(bf16[14,98,384]{2,1,0:T(8,128)(2,1)} %bitcast.6, bf16[14,98,384]{2,1,0:T(8,128)(2,1)} %bitcast.7, f32[4,104,128]{2,1,0:T(8,128)} %broadcast_in_dim.13.mask, f32[49,384]{1,0:T(8,128)} %reshape.68.dw_weight, ...), custom_call_target="tpu_custom_call" | custom-call | tf_op jit(solution)/shard_map/pallas_call | solution.py:574
  129.2 0.0 copy-start
  129.2 1.7 %copy-done = bf16[3,2,1536,128]{3,2,1,0:T(8,128)(2,1)S(1)} copy-done((bf16[3,2,1536,128]{3,2,1,0:T(8,128)(2,1)S(1)}, bf16[3,2,1536,128]{3,2,1,0:T(8,128)(2,1)}, u32[]{:S(2)}) %copy-start) | copy-done | bytes 2359320
  130.8 0.0 copy-start.1
  130.8 1.2 copy-done.1
  132.1 0.0 copy-start.2
  132.1 0.9 copy-done.2
  133.0 3.0 %shard_map.196 = (bf16[14,98,384]{2,1,0:T(8,128)(2,1)}, f32[7,7,384]{2,1,0:T(8,128)}, f32[1,384]{1,0:T(1,128)S(1)}, f32[1,384]{1,0:T(1,128)S(1)}, f32[1,384]{1,0...) custom-call(bf16[14,98,384]{2,1,0:T(8,128)(2,1)S(1)} %copy-done.1, ...), custom_call_target="tpu_custom_call" | custom-call | tf_op jit(solution)/shard_map/pallas_call | solution.py:621
  136.0 0.6 reduce
  136.6 0.6 reduce.1
  137.2 0.6 reduce.2
  137.8 0.6 reduce.4
  138.4 0.6 reduce.5
  139.0 0.6 reduce.3
  (2 shorter events, 0.0 us)
Async XLA Ops:
  129.2 1.7 %copy-start = (bf16[3,2,1536,128]{3,2,1,0:T(8,128)(2,1)S(1)}, bf16[3,2,1536,128]{3,2,1,0:T(8,128)(2,1)}, u32[]{:S(2)}) copy-start(bf16[3,2,1536,128]{3,2,1,0:T(8,128)(2,1)} %get-tuple-element.24.large) | copy-start | bytes 7077892
  130.8 1.2 copy-start.1
  132.1 0.9 copy-start.2
where the time goes:
time: 140 us
  Pallas kernels  121 us (86%)
  local copies, waits for them, and re-layouts  13.9 us (10%)
  other arithmetic  4.39 us (3%)
    pallas_call x1, Pallas kernels, run_block(): pl.pallas_call(block_kernel, out_shape=(jax.ShapeDtypeStruct((ROWS, BREAD...  118 us
    unnamed x7, local copies, waits for them, and re-layouts  3.82 us
    pallas_call x6, other arithmetic, finish(): pl.pallas_call(finish_kernel, out_shape=(jax.ShapeDtypeStruct(mixed.shape...  3.59 us
    pallas_call x1, Pallas kernels, finish(): pl.pallas_call(finish_kernel, out_shape=(jax.ShapeDtypeStruct(mixed.shape...  2.99 us

commit v1 on v0

--- a/solution.py
+++ b/solution.py
@@ -51,12 +51,21 @@
     return position, device_at({**where, axis: position})
 
 
+def stack_peer(where, distance):
+    place = (where["z"] * 2 + where["core"] + distance) % 16
+    return place, device_at({**where, "z": place // 2, "core": place % 2})
+
+
+def plane_peer(where, distance):
+    place = (where["y"] * 4 + where["x"] + distance) % 16
+    return place, device_at({**where, "y": place // 4, "x": place % 4})
+
+
 def enter(where):
     tile = lax.axis_index("tile")
-    peers = [device_at({**where, "core": 1 - where["core"]})]
-    peers += [(where["z"], (tile + step) % 32) for step in (1, 31)]
-    for axis, size in SIZES.items():
-        peers += [peer_along(where, axis, step)[1] for step in range(1, size)]
+    peers = [(where["z"], (tile + step) % 32) for step in (1, 31)]
+    for step in range(1, 16):
+        peers += [stack_peer(where, step)[1], plane_peer(where, step)[1]]
     barrier = pltpu.get_barrier_semaphore()
     for peer in peers:
         pl.semaphore_signal(barrier, inc=1, device_id=peer, device_id_type=MESH)
@@ -70,6 +79,7 @@
         self.heights = [rows]
         for axis in scatter:
             self.heights.append(self.heights[-1] // SIZES[axis])
+        self.phases = 2 * len(scatter) + len(exchange) + 3
         self.copies = 2 + 2 * sum(SIZES[a] - 1 for a in scatter) + sum(SIZES[a] - 1 for a in exchange)
 
     def scratch(self):
@@ -174,7 +184,7 @@
     def advance(self):
         phase, core = self.phase, self.where["core"]
         deep, wide = len(self.scatter), len(self.exchange)
-        if phase > 2 * deep + wide + 2:
+        if phase >= self.phases:
             return False
         self.phase += 1
         self.land()
@@ -210,8 +220,71 @@
         return False
 
 
+class Spread:
+    ROWS = 16
+    phases = 4
+
+    def scratch(self):
+        return [
+            pltpu.VMEM((15, self.ROWS, LANES), jnp.float32),
+            pltpu.VMEM((16, self.ROWS, LANES), jnp.float32),
+            pltpu.SemaphoreType.DMA((45,)),
+            pltpu.SemaphoreType.DMA((45,)),
+        ]
+
+    def bind(self, where, source, result, refs):
+        self.where, self.source, self.result = where, source, result
+        self.landed, self.slots, self.send_sems, self.recv_sems = refs
+        self.used, self.phase = 0, 0
+        self.flying, self.done = [], []
+        return self
+
+    copy = Sum.copy
+    land = Sum.land
+
+    def advance(self):
+        phase, where, rows = self.phase, self.where, self.ROWS
+        if phase >= self.phases:
+            return False
+        self.phase += 1
+        self.land()
+        place, flat = where["z"] * 2 + where["core"], where["y"] * 4 + where["x"]
+        mine = pl.ds(pl.multiple_of(place * rows, rows), rows)
+        if phase == 0:
+            for step in range(1, 16):
+                other, device = stack_peer(where, step)
+                block = self.source.at[pl.ds(pl.multiple_of(other * rows, rows), rows), :]
+                self.copy(block, self.landed.at[step - 1], device)
+        elif phase == 1:
+            total = self.source[mine, :]
+            for step in range(15):
+                total = total + self.landed[step]
+            self.slots[flat] = total
+            for step in range(1, 16):
+                _, device = plane_peer(where, step)
+                self.copy(self.slots.at[flat], self.slots.at[flat], device)
+        elif phase == 2:
+            total = self.slots[0]
+            for index in range(1, 16):
+                total = total + self.slots[index]
+            self.result[mine, :] = total
+            block = self.result.at[mine, :]
+            for step in range(1, 16):
+                _, device = stack_peer(where, step)
+                self.copy(block, block, device)
+        else:
+            for made in self.done:
+                made.wait_send()
+            return False
+        return True
+
+
 def lanes(group):
     return slice(group * LANES, (group + 1) * LANES)
+
+
+def line(vector, group):
+    return vector[lanes(group)].reshape(1, LANES)
 
 
 def by_eight(value):
@@ -226,6 +299,21 @@
     tail = density * series
     mass = jnp.where(pre_act >= 0.0, 1.0 - tail, tail)
     return pre_act * mass, mass + pre_act * density
+
+
+def spread_tissue(table, mask):
+    tile = lax.axis_index("tile")
+    mask[:, 96:WIDE, :] = jnp.zeros((4, WIDE - 96, LANES), jnp.float32)
+    for place in range(4):
+        row = jnp.clip(2 * tile - 1 + place, 0, 63)
+        inside = 1.0
+        if place == 0:
+            inside = jnp.where(tile > 0, 1.0, 0.0)
+        if place == 3:
+            inside = jnp.where(tile < 31, 1.0, 0.0)
+        for column in range(COLS):
+            live = jnp.where(table[row, column] >= 0, 1.0, 0.0) * inside
+            mask[place, column * TP : (column + 1) * TP, :] = jnp.full((TP, LANES), live, jnp.float32)
 
 
 def fill(feat, cot, mask, padded, cot_masked):
@@ -261,16 +349,18 @@
     lax.fori_loop(0, REACH, row, 0)
 
 
-def spread_taps(weight, taps):
+def spread_taps(weight, taps, bias, bias_rows):
+    for group in range(GROUPS):
+        bias_rows[group] = jnp.broadcast_to(line(bias, group), (8, LANES))
     for tap in range(K * K):
         for group in range(GROUPS):
-            taps[group, tap] = jnp.broadcast_to(weight[tap : tap + 1, lanes(group)], (8, LANES))
-
-
-def conv(padded, taps, bias, conv_out):
+            taps[group, tap] = jnp.broadcast_to(weight[tap // K, tap % K : tap % K + 1, lanes(group)], (8, LANES))
+
+
+def conv(padded, taps, bias_rows, conv_out):
     def tile(step, carry):
         group, column = step // 13, step % 13
-        total = jnp.zeros((ROWS, 8, LANES), jnp.float32) + bias[group]
+        total = jnp.zeros((ROWS, 8, LANES), jnp.float32) + bias_rows[group]
         for col_tap in range(K):
             window = padded[group, :, pl.ds(8 * column + 5 + col_tap, 8), :]
             for row_tap in range(K):
@@ -310,7 +400,7 @@
             centred = held[group] * inv
             conv_out[group, rows] = centred.reshape(2, WIDE, LANES)
             normed[place, lanes(group)] = (
-                centred * gain[:, lanes(group)] + offset[:, lanes(group)]
+                centred * line(gain, group) + line(offset, group)
             ).astype(jnp.bfloat16)
         return carry
 
@@ -322,7 +412,7 @@
         place = pl.ds(pl.multiple_of(step * PAIR, 16), PAIR)
         for group in range(GROUPS):
             pull = cot_masked[group, pl.ds(2 * step, 2)].reshape(PAIR, LANES)
-            pull = pull * (scale[:, lanes(group)] * LOSS_SCALE)
+            pull = pull * (line(scale, group) * LOSS_SCALE)
             grad_branch[place, lanes(group)] = pull.astype(jnp.bfloat16)
             sums[group] += by_eight(pull)
         return carry
@@ -352,7 +442,7 @@
     def block(step, carry):
         place = pl.ds(pl.multiple_of(step * PAIR, 16), PAIR)
         pre_act = jnp.dot(normed[place, :], w_in[:, units], preferred_element_type=jnp.float32)
-        pre_act = pre_act + b_in[:, units]
+        pre_act = pre_act + b_in[units].reshape(1, CHUNK)
         activ, slope = gelu_parts(pre_act)
         activ = activ.astype(jnp.bfloat16)
         hidden[place, :] = activ
@@ -363,7 +453,7 @@
         out = jnp.dot(activ, w_out[units, :], preferred_element_type=jnp.float32)
         back = nt(pull, w_in[:, units])
         if chunk == 0:
-            branch[place, :] = out + b_out[...]
+            branch[place, :] = out + b_out[...].reshape(1, C)
             grad_xn[place, :] = back
         else:
             branch[place, :] += out
@@ -382,7 +472,7 @@
         large[chunk, 1, group * CHUNK : (group + 1) * CHUNK, :] = second[:, lanes(group)]
 
 
-def after_mlp(branch, grad_xn, cot_masked, padded, centred, inv_std, mask, scale, gain, mixed, grad_conv, sums):
+def after_mlp(first, last, branch, grad_xn, cot_masked, padded, centred, inv_std, mask, scale, gain, mixed, grad_conv, sums):
     def row(i, carry):
         place = pl.ds(pl.multiple_of(i * WIDE, 8), WIDE)
         live = mask[1 + i // TP]
@@ -391,13 +481,13 @@
         for group in range(GROUPS):
             out = branch[place, lanes(group)].astype(jnp.bfloat16).astype(jnp.float32)
             sums[3 + group] += by_eight(cot_masked[group, i] * out)
-            kept = padded[group, i + REACH, 8 : 8 + WIDE, :] + live * (scale[:, lanes(group)] * out)
+            kept = padded[group, i + REACH, 8 : 8 + WIDE, :] + live * (line(scale, group) * out)
             mixed[i, :, lanes(group)] = kept[:BREADTH].astype(jnp.bfloat16)
             pull = grad_xn[place, lanes(group)].astype(jnp.bfloat16).astype(jnp.float32)
             cen = centred[group, i]
             sums[6 + group] += by_eight(pull * cen)
             sums[9 + group] += by_eight(pull)
-            pulls.append(pull * gain[:, lanes(group)])
+            pulls.append(pull * line(gain, group))
             held.append(cen)
         mean = jnp.sum(pulls[0] + pulls[1] + pulls[2], axis=-1, keepdims=True) * (1.0 / C)
         along = pulls[0] * held[0] + pulls[1] * held[1] + pulls[2] * held[2]
@@ -408,16 +498,14 @@
             sums[12 + group] += by_eight(pull)
         return carry
 
-    lax.fori_loop(0, ROWS, row, 0)
+    lax.fori_loop(first, last, row, 0)
 
 
 def collect(tap_sums, sums, in_sums, small):
     def put(place, value):
-        small[place // LANES, place % LANES : place % LANES + 1, :] = jnp.sum(
-            value, axis=0, keepdims=True
-        )
-
-    small[1, 40:LANES, :] = jnp.zeros((LANES - 40, LANES), jnp.float32)
+        small[place : place + 1, :] = jnp.sum(value, axis=0, keepdims=True)
+
+    small[168:, :] = jnp.zeros((2 * LANES - 168, LANES), jnp.float32)
     for group in range(GROUPS):
         for tap in range(K * K):
             put(group * K * K + tap, tap_sums[group, tap])
@@ -431,9 +519,9 @@
 def plan():
     large = [
         Sum(1536, jnp.bfloat16, scatter, exchange)
-        for scatter, exchange in ((("x", "z"), ("y",)), (("y", "z"), ("x",)), (("z", "y"), ("x",)))
+        for scatter, exchange in ((("z", "y"), ("x",)), (("y", "z"), ("x",)), (("x", "z"), ("y",)))
     ]
-    return large + [Sum(128, jnp.float32, ("z",), ("x", "y"))]
+    return large + [Spread()]
 
 
 def work_scratch():
@@ -465,16 +553,22 @@
         f32(GROUPS, K * K, 8, LANES),
         f32(GROUPS, ROWS, WIDE, LANES),
         f32(CHUNKS, 2, 1536, LANES),
-        f32(2, LANES, LANES),
+        f32(2 * LANES, LANES),
         b16(CHUNKS, 2, 1536, LANES),
-        f32(2, LANES, LANES),
+        f32(2 * LANES, LANES),
         b16(ROWS, BREADTH, C),
+        pltpu.SemaphoreType.DMA((5,)),
+        f32(4, WIDE, LANES),
+        f32(GROUPS, 8, LANES),
+        b16(ROWS, BREADTH, C),
+        b16(C, HID),
+        b16(HID, C),
         pltpu.SemaphoreType.DMA((3,)),
     ]
 
 
 def block_kernel(
-    feat, cot, mask, dw_weight, dw_bias, gain, offset, w_in, b_in, w_out, b_out, scale,
+    feat, cot_in, table, dw_weight, dw_bias, gain, offset, w_in_in, b_in, w_out_in, b_out, scale,
     mixed_out, large_out, small_out, *refs
 ):
     refs = list(refs)
@@ -483,10 +577,17 @@
         halo, halo_send, halo_recv, padded, cot_masked, taps, centred, inv_std, normed, grad_branch,
         normed_t, grad_branch_t, hidden, grad_pre, branch, grad_xn, in_sums, sums, tap_sums,
         grad_conv, large, small, large_held, small_held, mixed, out_sems,
+        mask, bias_rows, cot, w_in, w_out, in_sems,
     ) = refs[:own]
     refs = refs[own:]
     where = coordinates()
     core, tile = where["core"], lax.axis_index("tile")
+    loads = [
+        pltpu.make_async_copy(source, target, in_sems.at[index])
+        for index, (source, target) in enumerate(((cot_in, cot), (w_in_in, w_in), (w_out_in, w_out)))
+    ]
+    for made in loads:
+        made.start()
     enter(where)
     halves = []
     for side, step, first in ((0, 1, ROWS - REACH), (1, 31, 0)):
@@ -508,60 +609,77 @@
             keep, send = large.at[index, core], large.at[index, 1 - core]
             item.bind(where, keep, send, large_held.at[index], mine)
         else:
-            item.bind(where, small.at[core], small.at[1 - core], small_held, mine)
+            item.bind(where, small, small_held, mine)
         running.append(item)
+
+    copies = []
+
+    def store(source, target):
+        made = pltpu.make_async_copy(source, target, out_sems.at[len(copies)])
+        made.start()
+        copies.append(made)
 
     def advance(*which):
         for index in which:
-            running[index].advance()
-
-    fill(feat, cot, mask, padded, cot_masked)
-    spread_taps(dw_weight, taps)
+            item = running[index]
+            before = item.phase
+            if not item.advance() and item.phase > before:
+                if index < CHUNKS:
+                    store(large_held.at[index], large_out.at[index])
+                else:
+                    store(small_held, small_out)
+
+    spread_tissue(table, mask)
+    spread_taps(dw_weight, taps, dw_bias, bias_rows)
     sums[...] = jnp.zeros(sums.shape, jnp.float32)
     tap_sums[...] = jnp.zeros(tap_sums.shape, jnp.float32)
     in_sums[...] = jnp.zeros(in_sums.shape, jnp.float32)
     for rows in (normed, grad_branch, hidden, grad_pre):
         rows[CELLS:, :] = jnp.zeros((PADDED - CELLS, rows.shape[1]), jnp.bfloat16)
+    loads[0].wait()
+    fill(feat, cot, mask, padded, cot_masked)
     branch_grad(cot_masked, scale, grad_branch, sums)
     turn(grad_branch, grad_branch_t)
     for made in halves:
         made.wait_recv()
     fill_halo(halo, mask, padded)
-    conv(padded, taps, dw_bias, centred)
+    conv(padded, taps, bias_rows, centred)
     norm(centred, inv_std, gain, offset, normed)
     turn(normed, normed_t)
+    loads[1].wait()
+    loads[2].wait()
 
     work = (hidden, grad_pre, branch, grad_xn, in_sums)
     weights = (normed, grad_branch, w_in, b_in, w_out, b_out, work)
-    between = ((), (0,), (0, 1))
+    between = (((7, ()),), ((2, (0,)), (7, ())), ((2, (1,)), (5, (0,)), (7, ())))
+    ends = ((0,), (1,), (0, 1, 2))
     for chunk in range(CHUNKS):
-        mlp_rows(chunk, 0, 4, *weights)
-        advance(*between[chunk])
-        mlp_rows(chunk, 4, 7, *weights)
+        first = 0
+        for last, which in between[chunk]:
+            mlp_rows(chunk, first, last, *weights)
+            advance(*which)
+            first = last
         weight_grads(chunk, normed_t, grad_branch_t, hidden, grad_pre, large)
-        advance(*range(chunk + 1))
-    after_mlp(
-        branch, grad_xn, cot_masked, padded, centred, inv_std, mask, scale, gain, mixed, grad_conv, sums
-    )
-    mixed_copy = pltpu.make_async_copy(mixed, mixed_out, out_sems.at[0])
-    mixed_copy.start()
-    advance(0, 1, 2)
-    steps = (0, 10, 20, 30, 39)
-    for first, last in zip(steps, steps[1:]):
+        advance(*ends[chunk])
+    first = 0
+    for last, which in ((7, (2, 0)), (14, (0, 1))):
+        after_mlp(
+            first, last, branch, grad_xn, cot_masked, padded, centred, inv_std, mask, scale, gain, mixed,
+            grad_conv, sums,
+        )
+        advance(*which)
+        first = last
+    store(mixed, mixed_out)
+    first = 0
+    for last, which in ((7, (1,)), (12, (2,)), (16, (0,)), (20, (1,)), (26, (2,)), (30, (0, 2)), (35, (1, 2)), (39, ())):
         conv_grad(first, last, padded, grad_conv, tap_sums)
-        if last < 39:
-            advance(0, 1, 2)
+        advance(*which)
+        first = last
     collect(tap_sums, sums, in_sums, small)
-    going = [running[3], running[0], running[1], running[2]]
-    while going:
-        going = [item for item in going if item.advance()]
-    copies = [
-        pltpu.make_async_copy(large_held, large_out, out_sems.at[1]),
-        pltpu.make_async_copy(small_held, small_out, out_sems.at[2]),
-    ]
+    advance(3)
+    while any(item.phase < item.phases for item in running):
+        advance(2, 3, 0, 1)
     for made in copies:
-        made.start()
-    for made in copies + [mixed_copy]:
         made.wait()
     for made in halves:
         made.wait_send()
@@ -569,6 +687,9 @@
 
 def run_block(*operands):
     scratch = work_scratch()
+    spaces = [pltpu.VMEM] * len(operands)
+    spaces[1] = spaces[7] = spaces[9] = pl.ANY
+    spaces[2] = pltpu.SMEM
     for item in plan():
         scratch += item.scratch()
     return pl.pallas_call(
@@ -576,9 +697,9 @@
         out_shape=(
             jax.ShapeDtypeStruct((ROWS, BREADTH, C), jnp.bfloat16),
             jax.ShapeDtypeStruct((CHUNKS, 2, 1536, LANES), jnp.bfloat16),
-            jax.ShapeDtypeStruct((2, LANES, LANES), jnp.float32),
+            jax.ShapeDtypeStruct((2 * LANES, LANES), jnp.float32),
         ),
-        in_specs=[pl.BlockSpec(memory_space=pltpu.VMEM)] * len(operands),
+        in_specs=[pl.BlockSpec(memory_space=space) for space in spaces],
         out_specs=(pl.BlockSpec(memory_space=pl.ANY),) * 3,
         scratch_shapes=scratch,
         compiler_params=pltpu.CompilerParams(
@@ -587,54 +708,81 @@
     )(*operands)
 
 
-def finish_kernel(mixed_in, large, small, mixed, dw, dwb, ln_gain, ln_bias, w1, b1, w2, b2, scale):
-    mixed[...] = mixed_in[...]
-    for chunk in range(CHUNKS):
-        for group in range(CHUNK // LANES):
-            first = chunk * CHUNK + group * LANES
-            w1[:, first : first + LANES] = large[chunk, 0, group * C : (group + 1) * C, :].astype(
-                jnp.float32
-            )
-        for group in range(GROUPS):
-            w2[chunk * CHUNK : (chunk + 1) * CHUNK, lanes(group)] = large[
-                chunk, 1, group * CHUNK : (group + 1) * CHUNK, :
-            ].astype(jnp.float32)
+def finish_kernel(
+    mixed_in, large_in, small_in, mixed, dw, dwb, ln_gain, ln_bias, w1_out, b1, w2_out, b2, scale,
+    large, small, w1, w2, in_sems, out_sems
+):
+    across = pltpu.make_async_copy(mixed_in, mixed, out_sems.at[2 * CHUNKS])
+    little = pltpu.make_async_copy(small_in, small, in_sems.at[2 * CHUNKS])
+    pieces = [(chunk, half) for chunk in range(CHUNKS) for half in range(2)]
+    loads = [
+        pltpu.make_async_copy(large_in.at[piece], large.at[piece], in_sems.at[index])
+        for index, piece in enumerate(pieces)
+    ]
+    for made in [little] + loads + [across]:
+        made.start()
+    little.wait()
 
     def row(place):
-        return small[place // LANES, place % LANES : place % LANES + 1, :]
+        return small[place : place + 1, :]
 
     for group in range(GROUPS):
         for tap in range(K * K):
             dw[tap // K, tap % K : tap % K + 1, lanes(group)] = row(group * K * K + tap)
     for index, target in enumerate((b2, scale, ln_gain, ln_bias, dwb)):
         for group in range(GROUPS):
-            target[:, lanes(group)] = row(147 + index * GROUPS + group)
+            target[lanes(group)] = row(147 + index * GROUPS + group).reshape(LANES)
     for group in range(HID // LANES):
-        b1[:, lanes(group)] = row(162 + group)
+        b1[lanes(group)] = row(162 + group).reshape(LANES)
+
+    stores = []
+    for index, (chunk, half) in enumerate(pieces):
+        loads[index].wait()
+        units = slice(chunk * CHUNK, (chunk + 1) * CHUNK)
+        if half == 0:
+            for group in range(CHUNK // LANES):
+                first = chunk * CHUNK + group * LANES
+                w1[:, first : first + LANES] = large[
+                    chunk, 0, group * C : (group + 1) * C, :
+                ].astype(jnp.float32)
+            made = pltpu.make_async_copy(w1.at[:, units], w1_out.at[:, units], out_sems.at[index])
+        else:
+            for group in range(GROUPS):
+                w2[units, lanes(group)] = large[
+                    chunk, 1, group * CHUNK : (group + 1) * CHUNK, :
+                ].astype(jnp.float32)
+            made = pltpu.make_async_copy(w2.at[units, :], w2_out.at[units, :], out_sems.at[index])
+        made.start()
+        stores.append(made)
+    for made in stores + [across]:
+        made.wait()
 
 
 def finish(mixed, large, small):
     def f32(*shape):
         return jax.ShapeDtypeStruct(shape, jnp.float32)
 
-    vector = f32(1, C)
+    vector = f32(C)
+    spaces = [pltpu.VMEM] * 10
+    spaces[0] = spaces[5] = spaces[7] = pl.ANY
     return pl.pallas_call(
         finish_kernel,
         out_shape=(
             jax.ShapeDtypeStruct(mixed.shape, mixed.dtype), f32(K, K, C), vector, vector, vector,
-            f32(C, HID), f32(1, HID), f32(HID, C), vector, vector,
+            f32(C, HID), f32(HID), f32(HID, C), vector, vector,
         ),
-        in_specs=[pl.BlockSpec(memory_space=pltpu.VMEM)] * 3,
-        out_specs=(pl.BlockSpec(memory_space=pltpu.VMEM),) * 10,
-        compiler_params=pltpu.CompilerParams(vmem_limit_bytes=40 * 1024 * 1024),
+        in_specs=[pl.BlockSpec(memory_space=pl.ANY)] * 3,
+        out_specs=tuple(pl.BlockSpec(memory_space=space) for space in spaces),
+        scratch_shapes=[
+            pltpu.VMEM(large.shape, large.dtype),
+            pltpu.VMEM(small.shape, small.dtype),
+            pltpu.VMEM((C, HID), jnp.float32),
+            pltpu.VMEM((HID, C), jnp.float32),
+            pltpu.SemaphoreType.DMA((2 * CHUNKS + 1,)),
+            pltpu.SemaphoreType.DMA((2 * CHUNKS + 1,)),
+        ],
+        compiler_params=pltpu.CompilerParams(vmem_limit_bytes=60 * 1024 * 1024),
     )(mixed, large, small)
-
-
-def tissue_rows(table):
-    live = jnp.pad((table >= 0).astype(jnp.float32), ((1, 1), (0, 0)))
-    mine = lax.dynamic_slice_in_dim(live, lax.axis_index("tile") * 2, 4, 0)
-    cells = jnp.pad(jnp.repeat(mine, TP, axis=1), ((0, 0), (0, WIDE - BREADTH)))
-    return jnp.broadcast_to(cells[:, :, None], (4, WIDE, LANES))
 
 
 def local(
@@ -654,30 +802,19 @@
     mixed, large, small = run_block(
         features[0],
         cotangent[0],
-        tissue_rows(owner_slot[0]),
-        dw_weight.reshape(K * K, C),
-        dw_bias.reshape(GROUPS, 1, LANES),
-        ln_gain.reshape(1, C),
-        ln_bias.reshape(1, C),
+        owner_slot[0],
+        dw_weight,
+        dw_bias,
+        ln_gain,
+        ln_bias,
         w_in,
-        b_in.reshape(1, HID),
+        b_in,
         w_out,
-        b_out.reshape(1, C),
-        layer_scale.reshape(1, C),
+        b_out,
+        layer_scale,
     )
-    mixed, dw, dwb, gain, bias, w1, b1, w2, b2, scale = finish(mixed, large, small)
-    return (
-        mixed[None],
-        dw,
-        dwb.reshape(C),
-        gain.reshape(C),
-        bias.reshape(C),
-        w1,
-        b1.reshape(HID),
-        w2,
-        b2.reshape(C),
-        scale.reshape(C),
-    )
+    outs = finish(mixed, large, small)
+    return (outs[0][None],) + tuple(outs[1:])
 
 
 def solution(mesh):

time: 140 us -> 149 us (1.064)
  Pallas kernels: 121 us -> 147 us
  local copies, waits for them, and re-layouts: 13.9 us -> 1.4 us
  other arithmetic: 4.39 us -> 0 us
    pallas_call x1, Pallas kernels: 2.99 us -> 35.8 us  [finish(): pl.pallas_call(finish_kernel, out_shape=(jax.ShapeDtypeStruct(mixed.shape...]
    reshape x8 -> x0, local copies, waits for them, and re-layouts: 9.16 us -> none  [the longest x1 1.54 us: local(): dw_weight.reshape(K * K, C)]
    pallas_call x1, Pallas kernels: 118 us -> 111 us  [run_block(): pl.pallas_call(block_kernel, out_shape=(jax.ShapeDtypeStruct((ROWS, BREAD...]
    pallas_call x6 -> x0, other arithmetic: 3.59 us -> none  [finish(): pl.pallas_call(finish_kernel, out_shape=(jax.ShapeDtypeStruct(mixed.shape...]
    unnamed x7 -> x1, local copies, waits for them, and re-layouts: 3.82 us -> 1.4 us
where the time goes in v1:
time: 149 us
  Pallas kernels  147 us (99%)
    pallas_call x1, Pallas kernels, run_block(): pl.pallas_call(block_kernel, out_shape=(jax.ShapeDtypeStruct((ROWS, BREAD...  111 us
    pallas_call x1, Pallas kernels, finish(): pl.pallas_call(finish_kernel, out_shape=(jax.ShapeDtypeStruct(mixed.shape...  35.8 us

profile of v1, /device:TPU:1, one launch (start us, length us, event | category | flops | bytes accessed | tf_op | source)
XLA Modules:
  0.0 149.3 jit_solution(6740765099612195140)
XLA Ops:
  0.6 1.4 copy.22
  2.0 111.5 %shard_map.195 = (bf16[14,98,384]{2,1,0:T(8,128)(2,1)}, bf16[3,2,1536,128]{3,2,1,0:T(8,128)(2,1)}, f32[256,128]{1,0:T(8,128)}) custom-call(bf16[14,98,384]{2,1,0:T(8,128)(2,1)} %bitcast.4, bf16[14,98,384]{2,1,0:T(8,128)(2,1)} %bitcast.5, s32[64,14]{1,0:T(8,128)} %bitcast.6, f32[7,7,384]{2,1,0:T(8,128)} %dw_weight.1, f32[384]{0:T(512)} %dw_bias.1, f32[384]{0:T(512)} %gain.1, ...), custom_call_target="tpu_custom_call" | custom-call | tf_op jit(solution)/shard_map/pallas_call | solution.py:695
  113.5 35.8 %shard_map.196 = (bf16[14,98,384]{2,1,0:T(8,128)(2,1)}, f32[7,7,384]{2,1,0:T(8,128)}, f32[384]{0:T(512)}, f32[384]{0:T(512)}, f32[384]{0:T(512)}, /*index=5*/f32...) custom-call(bf16[14,98,384]{2,1,0:T(8,128)(2,1)} %get-tuple-element.23.mixed_in, ...), custom_call_target="tpu_custom_call" | custom-call | tf_op jit(solution)/shard_map/pallas_call | solution.py:768

commit v2 on v1

--- a/solution.py
+++ b/solution.py
@@ -22,6 +22,9 @@
 CHUNK = 512
 CHUNKS = HID // CHUNK
 PAIR = 2 * WIDE
+BLOCKS = CELLS // PAIR
+NORM_ROWS = 112
+STRIP = 16
 GROUPS = C // 128
 LOSS_SCALE = 1.0 / math.sqrt(8 * 32 * OWN * TP * TP)
 
@@ -321,7 +324,6 @@
     padded[:, :, 0:8, :] = edge
     padded[:, :, 104:112, :] = edge
     padded[:, :, 112:120, :] = edge
-    cot_masked[:, :, 96:104, :] = jnp.zeros((3, ROWS, 8, LANES), jnp.float32)
 
     def row(i, carry):
         live = mask[1 + i // TP][:BREADTH]
@@ -329,7 +331,10 @@
         pull = cot[i].astype(jnp.float32)
         for group in range(GROUPS):
             padded[group, i + REACH, 8 : 8 + BREADTH, :] = cells[:, lanes(group)] * live
-            cot_masked[group, i, 0:BREADTH, :] = pull[:, lanes(group)] * live
+            end = pl.ds(pl.multiple_of(i * WIDE + WIDE - 8, 8), 8)
+            cot_masked[group, end, :] = jnp.zeros((8, LANES), jnp.float32)
+            place = pl.ds(pl.multiple_of(i * WIDE, 8), BREADTH)
+            cot_masked[group, place, :] = pull[:, lanes(group)] * live
         return carry
 
     lax.fori_loop(0, ROWS, row, 0)
@@ -365,7 +370,8 @@
             window = padded[group, :, pl.ds(8 * column + 5 + col_tap, 8), :]
             for row_tap in range(K):
                 total = total + window[row_tap : row_tap + ROWS] * taps[group, row_tap * K + col_tap]
-        conv_out[group, :, pl.ds(pl.multiple_of(8 * column, 8), 8), :] = total
+        for i in range(ROWS):
+            conv_out[group, pl.ds(pl.multiple_of(i * WIDE + 8 * column, 8), 8), :] = total[i]
         return carry
 
     lax.fori_loop(0, GROUPS * 13, tile, 0)
@@ -374,7 +380,12 @@
 def conv_grad(first, last, padded, grad_conv, tap_sums):
     def tile(step, carry):
         group, column = step // 13, step % 13
-        pull = grad_conv[group, :, pl.ds(pl.multiple_of(8 * column, 8), 8), :]
+        pull = jnp.stack(
+            [
+                grad_conv[group, pl.ds(pl.multiple_of(i * WIDE + 8 * column, 8), 8), :]
+                for i in range(ROWS)
+            ]
+        )
         for col_tap in range(K):
             window = padded[group, :, pl.ds(8 * column + 5 + col_tap, 8), :]
             for row_tap in range(K):
@@ -386,38 +397,36 @@
 
 
 def norm(conv_out, inv_std, gain, offset, normed):
-    def pair(step, carry):
-        rows = pl.ds(2 * step, 2)
-        held = [conv_out[group, rows].reshape(PAIR, LANES) for group in range(GROUPS)]
+    def block(step, carry):
+        place = pl.ds(pl.multiple_of(step * NORM_ROWS, 16), NORM_ROWS)
+        held = [conv_out[group, place, :] for group in range(GROUPS)]
         mean = jnp.sum(held[0] + held[1] + held[2], axis=-1, keepdims=True) * (1.0 / C)
         held = [item - mean for item in held]
         squares = held[0] * held[0] + held[1] * held[1] + held[2] * held[2]
         var = jnp.sum(squares, axis=-1, keepdims=True) * (1.0 / C)
-        inv = jnp.broadcast_to(lax.rsqrt(var + 1e-06), (PAIR, LANES))
-        inv_std[rows] = inv.reshape(2, WIDE, LANES)
-        place = pl.ds(pl.multiple_of(step * PAIR, 16), PAIR)
+        inv = jnp.broadcast_to(lax.rsqrt(var + 1e-06), (NORM_ROWS, LANES))
+        inv_std[place, :] = inv
         for group in range(GROUPS):
             centred = held[group] * inv
-            conv_out[group, rows] = centred.reshape(2, WIDE, LANES)
+            conv_out[group, place, :] = centred
             normed[place, lanes(group)] = (
                 centred * line(gain, group) + line(offset, group)
             ).astype(jnp.bfloat16)
         return carry
 
-    lax.fori_loop(0, ROWS // 2, pair, 0)
+    lax.fori_loop(0, CELLS // NORM_ROWS, block, 0)
 
 
 def branch_grad(cot_masked, scale, grad_branch, sums):
-    def pair(step, carry):
-        place = pl.ds(pl.multiple_of(step * PAIR, 16), PAIR)
+    def block(step, carry):
+        place = pl.ds(pl.multiple_of(step * NORM_ROWS, 16), NORM_ROWS)
         for group in range(GROUPS):
-            pull = cot_masked[group, pl.ds(2 * step, 2)].reshape(PAIR, LANES)
-            pull = pull * (line(scale, group) * LOSS_SCALE)
+            pull = cot_masked[group, place, :] * (line(scale, group) * LOSS_SCALE)
             grad_branch[place, lanes(group)] = pull.astype(jnp.bfloat16)
             sums[group] += by_eight(pull)
         return carry
 
-    lax.fori_loop(0, ROWS // 2, pair, 0)
+    lax.fori_loop(0, CELLS // NORM_ROWS, block, 0)
 
 
 def turn(rows, turned):
@@ -435,32 +444,43 @@
     )
 
 
-def mlp_rows(chunk, first, last, normed, grad_branch, w_in, b_in, w_out, b_out, work):
-    hidden, grad_pre, branch, grad_xn, in_sums = work
+def rows_of(block):
+    return slice(block * PAIR, (block + 1) * PAIR)
+
+
+def mlp_enter(chunk, block, normed, grad_branch, w_in, w_out, pre_act, pull):
     units = slice(chunk * CHUNK, (chunk + 1) * CHUNK)
-
-    def block(step, carry):
-        place = pl.ds(pl.multiple_of(step * PAIR, 16), PAIR)
-        pre_act = jnp.dot(normed[place, :], w_in[:, units], preferred_element_type=jnp.float32)
-        pre_act = pre_act + b_in[units].reshape(1, CHUNK)
-        activ, slope = gelu_parts(pre_act)
-        activ = activ.astype(jnp.bfloat16)
-        hidden[place, :] = activ
-        pull = nt(grad_branch[place, :], w_out[units, :]) * slope
-        in_sums[:, units] += jnp.sum(pull.reshape(-1, 8, CHUNK), axis=0)
-        pull = pull.astype(jnp.bfloat16)
-        grad_pre[place, :] = pull
-        out = jnp.dot(activ, w_out[units, :], preferred_element_type=jnp.float32)
-        back = nt(pull, w_in[:, units])
-        if chunk == 0:
-            branch[place, :] = out + b_out[...].reshape(1, C)
-            grad_xn[place, :] = back
-        else:
-            branch[place, :] += out
-            grad_xn[place, :] += back
-        return carry
-
-    lax.fori_loop(first, last, block, 0)
+    place = rows_of(block)
+    pre_act[...] = jnp.dot(normed[place, :], w_in[:, units], preferred_element_type=jnp.float32)
+    pull[...] = nt(grad_branch[place, :], w_out[units, :])
+
+
+def mlp_strips(chunk, block, b_in, pre_act, pull, hidden, grad_pre, in_sums):
+    units = slice(chunk * CHUNK, (chunk + 1) * CHUNK)
+    bias = b_in[units].reshape(1, CHUNK)
+    total = in_sums[:, units]
+    for first in range(0, PAIR, STRIP):
+        strip = slice(first, first + STRIP)
+        place = slice(block * PAIR + first, block * PAIR + first + STRIP)
+        activ, slope = gelu_parts(pre_act[strip, :] + bias)
+        hidden[place, :] = activ.astype(jnp.bfloat16)
+        back = pull[strip, :] * slope
+        total = total + back[:8] + back[8:]
+        grad_pre[place, :] = back.astype(jnp.bfloat16)
+    in_sums[:, units] = total
+
+
+def mlp_leave(chunk, block, hidden, grad_pre, w_in, w_out, b_out, branch, grad_xn):
+    units = slice(chunk * CHUNK, (chunk + 1) * CHUNK)
+    place = rows_of(block)
+    out = jnp.dot(hidden[place, :], w_out[units, :], preferred_element_type=jnp.float32)
+    back = nt(grad_pre[place, :], w_in[:, units])
+    if chunk == 0:
+        branch[place, :] = out + b_out[...].reshape(1, C)
+        grad_xn[place, :] = back
+    else:
+        branch[place, :] += out
+        grad_xn[place, :] += back
 
 
 def weight_grads(chunk, normed_t, grad_branch_t, hidden, grad_pre, large):
@@ -473,18 +493,20 @@
 
 
 def after_mlp(first, last, branch, grad_xn, cot_masked, padded, centred, inv_std, mask, scale, gain, mixed, grad_conv, sums):
-    def row(i, carry):
-        place = pl.ds(pl.multiple_of(i * WIDE, 8), WIDE)
-        live = mask[1 + i // TP]
-        inv = inv_std[i]
+    def part(i, start, size):
+        place = pl.ds(pl.multiple_of(i * WIDE + start, 8), size)
+        live = mask[1 + i // TP, start : start + size]
+        used = min(BREADTH - start, size)
         pulls, held = [], []
         for group in range(GROUPS):
             out = branch[place, lanes(group)].astype(jnp.bfloat16).astype(jnp.float32)
-            sums[3 + group] += by_eight(cot_masked[group, i] * out)
-            kept = padded[group, i + REACH, 8 : 8 + WIDE, :] + live * (line(scale, group) * out)
-            mixed[i, :, lanes(group)] = kept[:BREADTH].astype(jnp.bfloat16)
+            sums[3 + group] += by_eight(cot_masked[group, place, :] * out)
+            kept = padded[group, i + REACH, 8 + start : 8 + start + size, :]
+            kept = kept + live * (line(scale, group) * out)
+            mixed[i, start : start + used, lanes(group)] = kept[:used].astype(jnp.bfloat16)
+        for group in range(GROUPS):
             pull = grad_xn[place, lanes(group)].astype(jnp.bfloat16).astype(jnp.float32)
-            cen = centred[group, i]
+            cen = centred[group, place, :]
             sums[6 + group] += by_eight(pull * cen)
             sums[9 + group] += by_eight(pull)
             pulls.append(pull * line(gain, group))
@@ -492,10 +514,15 @@
         mean = jnp.sum(pulls[0] + pulls[1] + pulls[2], axis=-1, keepdims=True) * (1.0 / C)
         along = pulls[0] * held[0] + pulls[1] * held[1] + pulls[2] * held[2]
         along = jnp.sum(along, axis=-1, keepdims=True) * (1.0 / C)
+        inv = inv_std[place, :]
         for group in range(GROUPS):
             pull = inv * (pulls[group] - mean - held[group] * along)
-            grad_conv[group, i] = pull
+            grad_conv[group, place, :] = pull
             sums[12 + group] += by_eight(pull)
+
+    def row(i, carry):
+        part(i, 0, 48)
+        part(i, 48, 56)
         return carry
 
     lax.fori_loop(first, last, row, 0)
@@ -536,22 +563,22 @@
         pltpu.SemaphoreType.DMA((2,)),
         pltpu.SemaphoreType.DMA((2,)),
         f32(GROUPS, ROWS + 2 * REACH, 120, LANES),
-        f32(GROUPS, ROWS, WIDE, LANES),
+        f32(GROUPS, CELLS, LANES),
         f32(GROUPS, K * K, 8, LANES),
-        f32(GROUPS, ROWS, WIDE, LANES),
-        f32(ROWS, WIDE, LANES),
+        f32(GROUPS, CELLS, LANES),
+        f32(CELLS, LANES),
         b16(PADDED, C),
         b16(PADDED, C),
         b16(C, PADDED),
         b16(C, PADDED),
-        b16(PADDED, CHUNK),
-        b16(PADDED, CHUNK),
+        b16(2, PADDED, CHUNK),
+        b16(2, PADDED, CHUNK),
         f32(CELLS, C),
         f32(CELLS, C),
         f32(8, HID),
         f32(15, 8, LANES),
         f32(GROUPS, K * K, 8, LANES),
-        f32(GROUPS, ROWS, WIDE, LANES),
+        f32(GROUPS, CELLS, LANES),
         f32(CHUNKS, 2, 1536, LANES),
         f32(2 * LANES, LANES),
         b16(CHUNKS, 2, 1536, LANES),
@@ -564,6 +591,8 @@
         b16(C, HID),
         b16(HID, C),
         pltpu.SemaphoreType.DMA((3,)),
+        f32(2, PAIR, CHUNK),
+        f32(2, PAIR, CHUNK),
     ]
 
 
@@ -577,7 +606,7 @@
         halo, halo_send, halo_recv, padded, cot_masked, taps, centred, inv_std, normed, grad_branch,
         normed_t, grad_branch_t, hidden, grad_pre, branch, grad_xn, in_sums, sums, tap_sums,
         grad_conv, large, small, large_held, small_held, mixed, out_sems,
-        mask, bias_rows, cot, w_in, w_out, in_sems,
+        mask, bias_rows, cot, w_in, w_out, in_sems, pre_act, pull,
     ) = refs[:own]
     refs = refs[own:]
     where = coordinates()
@@ -634,7 +663,7 @@
     sums[...] = jnp.zeros(sums.shape, jnp.float32)
     tap_sums[...] = jnp.zeros(tap_sums.shape, jnp.float32)
     in_sums[...] = jnp.zeros(in_sums.shape, jnp.float32)
-    for rows in (normed, grad_branch, hidden, grad_pre):
+    for rows in (normed, grad_branch, hidden.at[0], hidden.at[1], grad_pre.at[0], grad_pre.at[1]):
         rows[CELLS:, :] = jnp.zeros((PADDED - CELLS, rows.shape[1]), jnp.bfloat16)
     loads[0].wait()
     fill(feat, cot, mask, padded, cot_masked)
@@ -649,18 +678,46 @@
     loads[1].wait()
     loads[2].wait()
 
-    work = (hidden, grad_pre, branch, grad_xn, in_sums)
-    weights = (normed, grad_branch, w_in, b_in, w_out, b_out, work)
-    between = (((7, ()),), ((2, (0,)), (7, ())), ((2, (1,)), (5, (0,)), (7, ())))
-    ends = ((0,), (1,), (0, 1, 2))
-    for chunk in range(CHUNKS):
-        first = 0
-        for last, which in between[chunk]:
-            mlp_rows(chunk, first, last, *weights)
-            advance(*which)
-            first = last
-        weight_grads(chunk, normed_t, grad_branch_t, hidden, grad_pre, large)
-        advance(*ends[chunk])
+    steps = [(chunk, block) for chunk in range(CHUNKS) for block in range(BLOCKS)]
+
+    def enter_step(place):
+        if place < len(steps):
+            chunk, block = steps[place]
+            side = place % 2
+            mlp_enter(
+                chunk, block, normed, grad_branch, w_in, w_out, pre_act.at[side], pull.at[side]
+            )
+
+    def leave_step(place):
+        chunk, block = steps[place]
+        half = chunk % 2
+        mlp_leave(
+            chunk, block, hidden.at[half], grad_pre.at[half], w_in, w_out, b_out, branch, grad_xn
+        )
+
+    def finish_chunk(chunk):
+        half = chunk % 2
+        weight_grads(chunk, normed_t, grad_branch_t, hidden.at[half], grad_pre.at[half], large)
+
+    after_block = {
+        (1, 1): (0,), (1, 4): (0,), (2, 1): (0, 1), (2, 4): (1,), (2, 6): (0,)
+    }
+    enter_step(0)
+    for place, (chunk, block) in enumerate(steps):
+        half, side = chunk % 2, place % 2
+        enter_step(place + 1)
+        mlp_strips(
+            chunk, block, b_in, pre_act.at[side], pull.at[side], hidden.at[half], grad_pre.at[half],
+            in_sums,
+        )
+        if place > 0:
+            leave_step(place - 1)
+        if block == 0 and chunk > 0:
+            finish_chunk(chunk - 1)
+        advance(*after_block.get((chunk, block), ()))
+    leave_step(len(steps) - 1)
+    finish_chunk(CHUNKS - 1)
+    advance(2, 1)
     first = 0
     for last, which in ((7, (2, 0)), (14, (0, 1))):
         after_mlp(
@@ -710,16 +767,17 @@
 
 def finish_kernel(
     mixed_in, large_in, small_in, mixed, dw, dwb, ln_gain, ln_bias, w1_out, b1, w2_out, b2, scale,
-    large, small, w1, w2, in_sems, out_sems
+    large, small, w1, w2, held, in_sems, out_sems
 ):
-    across = pltpu.make_async_copy(mixed_in, mixed, out_sems.at[2 * CHUNKS])
+    arrive = pltpu.make_async_copy(mixed_in, held, in_sems.at[2 * CHUNKS + 1])
+    leave = pltpu.make_async_copy(held, mixed, out_sems.at[2 * CHUNKS])
     little = pltpu.make_async_copy(small_in, small, in_sems.at[2 * CHUNKS])
     pieces = [(chunk, half) for chunk in range(CHUNKS) for half in range(2)]
     loads = [
         pltpu.make_async_copy(large_in.at[piece], large.at[piece], in_sems.at[index])
         for index, piece in enumerate(pieces)
     ]
-    for made in [little] + loads + [across]:
+    for made in [little, arrive] + loads:
         made.start()
     little.wait()
 
@@ -735,6 +793,8 @@
     for group in range(HID // LANES):
         b1[lanes(group)] = row(162 + group).reshape(LANES)
 
+    arrive.wait()
+    leave.start()
     stores = []
     for index, (chunk, half) in enumerate(pieces):
         loads[index].wait()
@@ -754,7 +814,7 @@
             made = pltpu.make_async_copy(w2.at[units, :], w2_out.at[units, :], out_sems.at[index])
         made.start()
         stores.append(made)
-    for made in stores + [across]:
+    for made in stores + [leave]:
         made.wait()
 
 
@@ -778,7 +838,8 @@
             pltpu.VMEM(small.shape, small.dtype),
             pltpu.VMEM((C, HID), jnp.float32),
             pltpu.VMEM((HID, C), jnp.float32),
-            pltpu.SemaphoreType.DMA((2 * CHUNKS + 1,)),
+            pltpu.VMEM(mixed.shape, mixed.dtype),
+            pltpu.SemaphoreType.DMA((2 * CHUNKS + 2,)),
             pltpu.SemaphoreType.DMA((2 * CHUNKS + 1,)),
         ],
         compiler_params=pltpu.CompilerParams(vmem_limit_bytes=60 * 1024 * 1024),

time: 149 us -> 120 us (0.81)
  Pallas kernels: 147 us -> 118 us
    pallas_call x1, Pallas kernels: 35.8 us -> 4.63 us  [finish(): pl.pallas_call(finish_kernel, out_shape=(jax.ShapeDtypeStruct(mixed.shape...]
    pallas_call x1, Pallas kernels: 111 us -> 113 us  [run_block(): pl.pallas_call(block_kernel, out_shape=(jax.ShapeDtypeStruct((ROWS, BREAD...]
where the time goes in v2:
time: 120 us
  Pallas kernels  118 us (98%)
  local copies, waits for them, and re-layouts  1.4 us (1%)
    pallas_call x1, Pallas kernels, run_block(): pl.pallas_call(block_kernel, out_shape=(jax.ShapeDtypeStruct((ROWS, BREAD...  113 us
    pallas_call x1, Pallas kernels, finish(): pl.pallas_call(finish_kernel, out_shape=(jax.ShapeDtypeStruct(mixed.shape...  4.63 us

profile of v2, /device:TPU:1, one launch (start us, length us, event | category | flops | bytes accessed | tf_op | source)
XLA Modules:
  0.0 120.0 jit_solution(9124690288186823670)
XLA Ops:
  0.6 1.4 %copy.22 = s32[1,64,14]{2,1,0:T(8,128)} copy(s32[1,64,14]{1,0,2:T(1,128)} %param.14) | data formatting | bytes 7168 | tf_op args[2]
  2.0 113.2 %shard_map.195 = (bf16[14,98,384]{2,1,0:T(8,128)(2,1)}, bf16[3,2,1536,128]{3,2,1,0:T(8,128)(2,1)}, f32[256,128]{1,0:T(8,128)}) custom-call(bf16[14,98,384]{2,1,0:T(8,128)(2,1)} %bitcast.4, bf16[14,98,384]{2,1,0:T(8,128)(2,1)} %bitcast.5, s32[64,14]{1,0:T(8,128)} %bitcast.6, f32[7,7,384]{2,1,0:T(8,128)} %dw_weight.1, f32[384]{0:T(512)} %dw_bias.1, f32[384]{0:T(512)} %gain.1, ...), custom_call_target="tpu_custom_call" | custom-call | tf_op jit(solution)/shard_map/pallas_call | solution.py:752
  115.2 4.6 %shard_map.196 = (bf16[14,98,384]{2,1,0:T(8,128)(2,1)}, f32[7,7,384]{2,1,0:T(8,128)}, f32[384]{0:T(512)}, f32[384]{0:T(512)}, f32[384]{0:T(512)}, /*index=5*/f32...) custom-call(bf16[14,98,384]{2,1,0:T(8,128)(2,1)} %get-tuple-element.23.mixed_in, ...), custom_call_target="tpu_custom_call" | custom-call | tf_op jit(solution)/shard_map/pallas_call | solution.py:828

commit v3 on v2

--- a/solution.py
+++ b/solution.py
@@ -551,73 +551,57 @@
     return large + [Spread()]
 
 
-def work_scratch():
-    def f32(*shape):
-        return pltpu.VMEM(shape, jnp.float32)
-
-    def b16(*shape):
-        return pltpu.VMEM(shape, jnp.bfloat16)
-
-    return [
-        b16(2, REACH, BREADTH, C),
-        pltpu.SemaphoreType.DMA((2,)),
-        pltpu.SemaphoreType.DMA((2,)),
-        f32(GROUPS, ROWS + 2 * REACH, 120, LANES),
-        f32(GROUPS, CELLS, LANES),
-        f32(GROUPS, K * K, 8, LANES),
-        f32(GROUPS, CELLS, LANES),
-        f32(CELLS, LANES),
-        b16(PADDED, C),
-        b16(PADDED, C),
-        b16(C, PADDED),
-        b16(C, PADDED),
-        b16(2, PADDED, CHUNK),
-        b16(2, PADDED, CHUNK),
-        f32(CELLS, C),
-        f32(CELLS, C),
-        f32(8, HID),
-        f32(15, 8, LANES),
-        f32(GROUPS, K * K, 8, LANES),
-        f32(GROUPS, CELLS, LANES),
-        f32(CHUNKS, 2, 1536, LANES),
-        f32(2 * LANES, LANES),
-        b16(CHUNKS, 2, 1536, LANES),
-        f32(2 * LANES, LANES),
-        b16(ROWS, BREADTH, C),
-        pltpu.SemaphoreType.DMA((5,)),
-        f32(4, WIDE, LANES),
-        f32(GROUPS, 8, LANES),
-        b16(ROWS, BREADTH, C),
-        b16(C, HID),
-        b16(HID, C),
-        pltpu.SemaphoreType.DMA((3,)),
-        f32(2, PAIR, CHUNK),
-        f32(2, PAIR, CHUNK),
-    ]
-
-
-def block_kernel(
-    feat, cot_in, table, dw_weight, dw_bias, gain, offset, w_in_in, b_in, w_out_in, b_out, scale,
-    mixed_out, large_out, small_out, *refs
+F32, B16 = jnp.float32, jnp.bfloat16
+FORWARD = (
+    ((GROUPS, ROWS + 2 * REACH, 120, LANES), F32),
+    ((GROUPS, CELLS, LANES), F32),
+    ((GROUPS, CELLS, LANES), F32),
+    ((CELLS, LANES), F32),
+    ((PADDED, C), B16),
+    ((PADDED, C), B16),
+    ((C, PADDED), B16),
+    ((C, PADDED), B16),
+    ((15, 8, LANES), F32),
+    ((4, WIDE, LANES), F32),
+)
+MIDDLE = (
+    ((CHUNKS, 2, 1536, LANES), F32),
+    ((CELLS, C), F32),
+    ((CELLS, C), F32),
+    ((8, HID), F32),
+)
+LAST = (
+    ((ROWS, BREADTH, C), B16),
+    ((CHUNKS, 2, 1536, LANES), B16),
+    ((2 * LANES, LANES), F32),
+)
+
+
+def shapes_of(layout):
+    return tuple(jax.ShapeDtypeStruct(shape, dtype) for shape, dtype in layout)
+
+
+def vmem(layout):
+    return [pltpu.VMEM(shape, dtype) for shape, dtype in layout]
+
+
+def enter_forward(where):
+    tile = lax.axis_index("tile")
+    barrier = pltpu.get_barrier_semaphore()
+    for step in (1, 31):
+        peer = (where["z"], (tile + step) % 32)
+        pl.semaphore_signal(barrier, inc=1, device_id=peer, device_id_type=MESH)
+    pl.semaphore_wait(barrier, 2)
+
+
+def forward_kernel(
+    feat, cot, table, dw_weight, dw_bias, gain, offset, scale,
+    padded, cot_masked, centred, inv_std, normed, grad_branch, normed_t, grad_branch_t, sums, mask,
+    halo, halo_send, halo_recv, taps, bias_rows,
 ):
-    refs = list(refs)
-    own = len(work_scratch())
-    (
-        halo, halo_send, halo_recv, padded, cot_masked, taps, centred, inv_std, normed, grad_branch,
-        normed_t, grad_branch_t, hidden, grad_pre, branch, grad_xn, in_sums, sums, tap_sums,
-        grad_conv, large, small, large_held, small_held, mixed, out_sems,
-        mask, bias_rows, cot, w_in, w_out, in_sems, pre_act, pull,
-    ) = refs[:own]
-    refs = refs[own:]
     where = coordinates()
-    core, tile = where["core"], lax.axis_index("tile")
-    loads = [
-        pltpu.make_async_copy(source, target, in_sems.at[index])
-        for index, (source, target) in enumerate(((cot_in, cot), (w_in_in, w_in), (w_out_in, w_out)))
-    ]
-    for made in loads:
-        made.start()
-    enter(where)
+    tile = lax.axis_index("tile")
+    enter_forward(where)
     halves = []
     for side, step, first in ((0, 1, ROWS - REACH), (1, 31, 0)):
         made = pltpu.make_async_remote_copy(
@@ -630,42 +614,11 @@
         )
         made.start()
         halves.append(made)
-    running = []
-    for index, item in enumerate(plan()):
-        count = len(item.scratch())
-        mine, refs = refs[:count], refs[count:]
-        if index < CHUNKS:
-            keep, send = large.at[index, core], large.at[index, 1 - core]
-            item.bind(where, keep, send, large_held.at[index], mine)
-        else:
-            item.bind(where, small, small_held, mine)
-        running.append(item)
-
-    copies = []
-
-    def store(source, target):
-        made = pltpu.make_async_copy(source, target, out_sems.at[len(copies)])
-        made.start()
-        copies.append(made)
-
-    def advance(*which):
-        for index in which:
-            item = running[index]
-            before = item.phase
-            if not item.advance() and item.phase > before:
-                if index < CHUNKS:
-                    store(large_held.at[index], large_out.at[index])
-                else:
-                    store(small_held, small_out)
-
     spread_tissue(table, mask)
     spread_taps(dw_weight, taps, dw_bias, bias_rows)
     sums[...] = jnp.zeros(sums.shape, jnp.float32)
-    tap_sums[...] = jnp.zeros(tap_sums.shape, jnp.float32)
-    in_sums[...] = jnp.zeros(in_sums.shape, jnp.float32)
-    for rows in (normed, grad_branch, hidden.at[0], hidden.at[1], grad_pre.at[0], grad_pre.at[1]):
+    for rows in (normed, grad_branch):
         rows[CELLS:, :] = jnp.zeros((PADDED - CELLS, rows.shape[1]), jnp.bfloat16)
-    loads[0].wait()
     fill(feat, cot, mask, padded, cot_masked)
     branch_grad(cot_masked, scale, grad_branch, sums)
     turn(grad_branch, grad_branch_t)
@@ -675,9 +628,18 @@
     conv(padded, taps, bias_rows, centred)
     norm(centred, inv_std, gain, offset, normed)
     turn(normed, normed_t)
-    loads[1].wait()
-    loads[2].wait()
-
+    for made in halves:
+        made.wait_send()
+
+
+def mlp_kernel(
+    normed, grad_branch, normed_t, grad_branch_t, w_in, b_in, w_out, b_out,
+    large, branch, grad_xn, in_sums,
+    hidden, grad_pre, pre_act, pull,
+):
+    in_sums[...] = jnp.zeros(in_sums.shape, jnp.float32)
+    for rows in (hidden.at[0], hidden.at[1], grad_pre.at[0], grad_pre.at[1]):
+        rows[CELLS:, :] = jnp.zeros((PADDED - CELLS, rows.shape[1]), jnp.bfloat16)
     steps = [(chunk, block) for chunk in range(CHUNKS) for block in range(BLOCKS)]
 
     def enter_step(place):
@@ -699,9 +661,6 @@
         half = chunk % 2
         weight_grads(chunk, normed_t, grad_branch_t, hidden.at[half], grad_pre.at[half], large)
 
-    after_block = {
-        (1, 1): (0,), (1, 4): (0,), (2, 1): (0, 1), (2, 4): (1,), (2, 6): (0,)
-    }
     enter_step(0)
     for place, (chunk, block) in enumerate(steps):
         half, side = chunk % 2, place % 2
@@ -714,12 +673,52 @@
             leave_step(place - 1)
         if block == 0 and chunk > 0:
             finish_chunk(chunk - 1)
-        advance(*after_block.get((chunk, block), ()))
     leave_step(len(steps) - 1)
     finish_chunk(CHUNKS - 1)
-    advance(2, 1)
+
+
+def tail_kernel(
+    padded, cot_masked, centred, inv_std, first_sums, mask, large, branch, grad_xn, in_sums, gain, scale,
+    mixed_out, large_out, small_out,
+    mixed, large_held, small_held, sums, tap_sums, grad_conv, small, out_sems, *refs
+):
+    refs = list(refs)
+    where = coordinates()
+    core = where["core"]
+    enter(where)
+    running = []
+    for index, item in enumerate(plan()):
+        count = len(item.scratch())
+        mine, refs = refs[:count], refs[count:]
+        if index < CHUNKS:
+            keep, send = large.at[index, core], large.at[index, 1 - core]
+            item.bind(where, keep, send, large_held.at[index], mine)
+        else:
+            item.bind(where, small, small_held, mine)
+        running.append(item)
+    copies = []
+
+    def store(source, target):
+        made = pltpu.make_async_copy(source, target, out_sems.at[len(copies)])
+        made.start()
+        copies.append(made)
+
+    def advance(*which):
+        for index in which:
+            item = running[index]
+            before = item.phase
+            if not item.advance() and item.phase > before:
+                if index < CHUNKS:
+                    store(large_held.at[index], large_out.at[index])
+                else:
+                    store(small_held, small_out)
+
+    advance(0, 1, 2)
+    sums[...] = first_sums[...]
+    tap_sums[...] = jnp.zeros(tap_sums.shape, jnp.float32)
+    advance(0, 1, 2)
     first = 0
-    for last, which in ((7, (2, 0)), (14, (0, 1))):
+    for last, which in ((7, ()), (14, (0, 1, 2))):
         after_mlp(
             first, last, branch, grad_xn, cot_masked, padded, centred, inv_std, mask, scale, gain, mixed,
             grad_conv, sums,
@@ -728,7 +727,7 @@
         first = last
     store(mixed, mixed_out)
     first = 0
-    for last, which in ((7, (1,)), (12, (2,)), (16, (0,)), (20, (1,)), (26, (2,)), (30, (0, 2)), (35, (1, 2)), (39, ())):
+    for last, which in ((10, (0, 1, 2)), (18, (0, 1, 2)), (28, (0, 1, 2)), (39, ())):
         conv_grad(first, last, padded, grad_conv, tap_sums)
         advance(*which)
         first = last
@@ -738,31 +737,62 @@
         advance(2, 3, 0, 1)
     for made in copies:
         made.wait()
-    for made in halves:
-        made.wait_send()
-
-
-def run_block(*operands):
-    scratch = work_scratch()
-    spaces = [pltpu.VMEM] * len(operands)
-    spaces[1] = spaces[7] = spaces[9] = pl.ANY
+
+
+def call(kernel, outs, out_spaces, spaces, scratch, collective, operands):
+    remote = {} if collective is None else {"collective_id": collective, "has_side_effects": True}
+    return pl.pallas_call(
+        kernel,
+        out_shape=outs,
+        in_specs=[pl.BlockSpec(memory_space=space) for space in spaces],
+        out_specs=tuple(pl.BlockSpec(memory_space=space) for space in out_spaces),
+        scratch_shapes=scratch,
+        compiler_params=pltpu.CompilerParams(vmem_limit_bytes=60 * 1024 * 1024, **remote),
+    )(*operands)
+
+
+def run_block(
+    feat, cot, table, dw_weight, dw_bias, gain, offset, w_in, b_in, w_out, b_out, scale
+):
+    spaces = [pltpu.VMEM] * 8
     spaces[2] = pltpu.SMEM
+    padded, cot_masked, centred, inv_std, normed, grad_branch, normed_t, grad_branch_t, sums, mask = call(
+        forward_kernel, shapes_of(FORWARD), [pltpu.VMEM] * len(FORWARD), spaces,
+        [
+            pltpu.VMEM((2, REACH, BREADTH, C), B16),
+            pltpu.SemaphoreType.DMA((2,)),
+            pltpu.SemaphoreType.DMA((2,)),
+            pltpu.VMEM((GROUPS, K * K, 8, LANES), F32),
+            pltpu.VMEM((GROUPS, 8, LANES), F32),
+        ],
+        1, (feat, cot, table, dw_weight, dw_bias, gain, offset, scale),
+    )
+    large, branch, grad_xn, in_sums = call(
+        mlp_kernel, shapes_of(MIDDLE), [pltpu.VMEM] * len(MIDDLE), [pltpu.VMEM] * 8,
+        [
+            pltpu.VMEM((2, PADDED, CHUNK), B16),
+            pltpu.VMEM((2, PADDED, CHUNK), B16),
+            pltpu.VMEM((2, PAIR, CHUNK), F32),
+            pltpu.VMEM((2, PAIR, CHUNK), F32),
+        ],
+        None, (normed, grad_branch, normed_t, grad_branch_t, w_in, b_in, w_out, b_out),
+    )
+    scratch = vmem(LAST) + [
+        pltpu.VMEM((15, 8, LANES), F32),
+        pltpu.VMEM((GROUPS, K * K, 8, LANES), F32),
+        pltpu.VMEM((GROUPS, CELLS, LANES), F32),
+        pltpu.VMEM((2 * LANES, LANES), F32),
+        pltpu.SemaphoreType.DMA((5,)),
+    ]
     for item in plan():
         scratch += item.scratch()
-    return pl.pallas_call(
-        block_kernel,
-        out_shape=(
-            jax.ShapeDtypeStruct((ROWS, BREADTH, C), jnp.bfloat16),
-            jax.ShapeDtypeStruct((CHUNKS, 2, 1536, LANES), jnp.bfloat16),
-            jax.ShapeDtypeStruct((2 * LANES, LANES), jnp.float32),
-        ),
-        in_specs=[pl.BlockSpec(memory_space=space) for space in spaces],
-        out_specs=(pl.BlockSpec(memory_space=pl.ANY),) * 3,
-        scratch_shapes=scratch,
-        compiler_params=pltpu.CompilerParams(
-            collective_id=0, has_side_effects=True, vmem_limit_bytes=60 * 1024 * 1024
-        ),
-    )(*operands)
+    operands = (
+        padded, cot_masked, centred, inv_std, sums, mask, large, branch, grad_xn, in_sums, gain, scale
+    )
+    return call(
+        tail_kernel, shapes_of(LAST), [pl.ANY] * len(LAST), [pltpu.VMEM] * len(operands), scratch, 0,
+        operands,
+    )
 
 
 def finish_kernel(

time: 120 us -> 130 us (1.083)
  Pallas kernels: 118 us -> 128 us
    pallas_call x1 -> x3, Pallas kernels: 113 us -> 123 us  [call(): pl.pallas_call(kernel, out_shape=outs, in_specs=[pl.BlockSpec(memory_spac...]
where the time goes in v3:
time: 130 us
  Pallas kernels  128 us (98%)
  local copies, waits for them, and re-layouts  1.4 us (1%)
    pallas_call x3, Pallas kernels, call(): pl.pallas_call(kernel, out_shape=outs, in_specs=[pl.BlockSpec(memory_spac...  123 us
    pallas_call x1, Pallas kernels, finish(): pl.pallas_call(finish_kernel, out_shape=(jax.ShapeDtypeStruct(mixed.shape...  4.63 us

profile of v3, /device:TPU:1, one launch (start us, length us, event | category | flops | bytes accessed | tf_op | source)
XLA Modules:
  0.0 130.2 jit_solution(16931989930916934131)
XLA Ops:
  0.6 1.4 %copy.22 = s32[1,64,14]{2,1,0:T(8,128)} copy(s32[1,64,14]{1,0,2:T(1,128)} %param.14) | data formatting | bytes 7168 | tf_op args[2]
  2.0 28.0 %shard_map.195 = (f32[3,20,120,128]{3,2,1,0:T(8,128)}, f32[3,1456,128]{2,1,0:T(8,128)}, f32[3,1456,128]{2,1,0:T(8,128)}, f32[1456,128]{1,0:T(8,128)}, bf16[1536,...) custom-call(bf16[14,98,384]{2,1,0:T(8,128)(2,1)} %bitcast.4, ...), custom_call_target="tpu_custom_call" | custom-call | tf_op jit(solution)/shard_map/pallas_call | solution.py:744
  30.1 23.6 %shard_map.196 = (f32[3,2,1536,128]{3,2,1,0:T(8,128)}, f32[1456,384]{1,0:T(8,128)}, f32[1456,384]{1,0:T(8,128)}, f32[8,1536]{1,0:T(8,128)}) custom-call(bf16[1536,384]{1,0:T(8,128)(2,1)} %get-tuple-element.43.normed, bf16[1536,384]{1,0:T(8,128)(2,1)} %get-tuple-element.44.grad_branch, bf16[384,1536]{1,0:T(8,128)(2,1)} %get-tuple-element.45.normed_t, ...), custom_call_target="tpu_custom_call" | custom-call | tf_op jit(solution)/shard_map/pallas_call | solution.py:744
  53.7 71.7 %shard_map.197 = (bf16[14,98,384]{2,1,0:T(8,128)(2,1)}, bf16[3,2,1536,128]{3,2,1,0:T(8,128)(2,1)}, f32[256,128]{1,0:T(8,128)}) custom-call(f32[3,20,120,128]{3,2,1,0:T(8,128)} %get-tuple-element.37.padded, f32[3,1456,128]{2,1,0:T(8,128)} %get-tuple-element.38.cot_masked, f32[3,1456,128]{2,1,0:T(8,128)} %get-tuple-element.39.centred, ...), custom_call_target="tpu_custom_call" | custom-call | tf_op jit(solution)/shard_map/pallas_call | solution.py:744
  125.4 4.6 %shard_map.198 = (bf16[14,98,384]{2,1,0:T(8,128)(2,1)}, f32[7,7,384]{2,1,0:T(8,128)}, f32[384]{0:T(512)}, f32[384]{0:T(512)}, f32[384]{0:T(512)}, /*index=5*/f32...) custom-call(bf16[14,98,384]{2,1,0:T(8,128)(2,1)} %get-tuple-element.51.mixed_in, ...), custom_call_target="tpu_custom_call" | custom-call | tf_op jit(solution)/shard_map/pallas_call | solution.py:858

commit v4 on v2

--- a/solution.py
+++ b/solution.py
@@ -315,7 +315,7 @@
         if place == 3:
             inside = jnp.where(tile < 31, 1.0, 0.0)
         for column in range(COLS):
-            live = jnp.where(table[row, column] >= 0, 1.0, 0.0) * inside
+            live = jnp.where(table[column, row] >= 0, 1.0, 0.0) * inside
             mask[place, column * TP : (column + 1) * TP, :] = jnp.full((TP, LANES), live, jnp.float32)
 
 
@@ -528,27 +528,38 @@
     lax.fori_loop(first, last, row, 0)
 
 
-def collect(tap_sums, sums, in_sums, small):
-    def put(place, value):
-        small[place : place + 1, :] = jnp.sum(value, axis=0, keepdims=True)
-
+def put(small, place, value):
+    small[place : place + 1, :] = jnp.sum(value, axis=0, keepdims=True)
+
+
+def collect_vectors(sums, in_sums, small):
     small[168:, :] = jnp.zeros((2 * LANES - 168, LANES), jnp.float32)
+    for index in range(15):
+        value = sums[index]
+        put(small, 147 + index, value * LOSS_SCALE if 3 <= index < 6 else value)
+    for group in range(HID // LANES):
+        put(small, 162 + group, in_sums[:, lanes(group)])
+
+
+def collect_taps(tap_sums, small):
     for group in range(GROUPS):
         for tap in range(K * K):
-            put(group * K * K + tap, tap_sums[group, tap])
-    for index in range(15):
-        value = sums[index]
-        put(147 + index, value * LOSS_SCALE if 3 <= index < 6 else value)
-    for group in range(HID // LANES):
-        put(162 + group, in_sums[:, lanes(group)])
+            put(small, group * K * K + tap, tap_sums[group, tap])
+
+
+X_FIRST, Y_FIRST = (("x", "z"), ("y",)), (("y", "z"), ("x",))
+PIECES = (
+    (0, 0, 1024, X_FIRST),
+    (0, 1024, 512, Y_FIRST),
+    (1, 0, 1024, Y_FIRST),
+    (1, 1024, 512, X_FIRST),
+    (2, 0, 1024, X_FIRST),
+    (2, 1024, 512, Y_FIRST),
+)
 
 
 def plan():
-    large = [
-        Sum(1536, jnp.bfloat16, scatter, exchange)
-        for scatter, exchange in ((("z", "y"), ("x",)), (("y", "z"), ("x",)), (("x", "z"), ("y",)))
-    ]
-    return large + [Spread()]
+    return [Sum(rows, jnp.bfloat16, *order) for _, _, rows, order in PIECES] + [Spread()]
 
 
 def work_scratch():
@@ -584,7 +595,7 @@
         b16(CHUNKS, 2, 1536, LANES),
         f32(2 * LANES, LANES),
         b16(ROWS, BREADTH, C),
-        pltpu.SemaphoreType.DMA((5,)),
+        pltpu.SemaphoreType.DMA((len(PIECES) + 2,)),
         f32(4, WIDE, LANES),
         f32(GROUPS, 8, LANES),
         b16(ROWS, BREADTH, C),
@@ -634,9 +645,11 @@
     for index, item in enumerate(plan()):
         count = len(item.scratch())
         mine, refs = refs[:count], refs[count:]
-        if index < CHUNKS:
-            keep, send = large.at[index, core], large.at[index, 1 - core]
-            item.bind(where, keep, send, large_held.at[index], mine)
+        if index < len(PIECES):
+            chunk, start, rows, _ = PIECES[index]
+            span = pl.ds(start, rows)
+            keep, send = large.at[chunk, core, span, :], large.at[chunk, 1 - core, span, :]
+            item.bind(where, keep, send, large_held.at[chunk, :, span, :], mine)
         else:
             item.bind(where, small, small_held, mine)
         running.append(item)
@@ -649,12 +662,14 @@
         copies.append(made)
 
     def advance(*which):
-        for index in which:
-            item = running[index]
+        for index, item in enumerate(running):
+            chunk = PIECES[index][0] if index < len(PIECES) else CHUNKS
             before = item.phase
-            if not item.advance() and item.phase > before:
-                if index < CHUNKS:
-                    store(large_held.at[index], large_out.at[index])
+            if chunk in which and not item.advance() and item.phase > before:
+                if chunk < CHUNKS:
+                    _, start, rows, _ = PIECES[index]
+                    span = pl.ds(start, rows)
+                    store(large_held.at[chunk, :, span, :], large_out.at[chunk, :, span, :])
                 else:
                     store(small_held, small_out)
 
@@ -700,7 +715,7 @@
         weight_grads(chunk, normed_t, grad_branch_t, hidden.at[half], grad_pre.at[half], large)
 
     after_block = {
-        (1, 1): (0,), (1, 4): (0,), (2, 1): (0, 1), (2, 4): (1,), (2, 6): (0,)
+        (1, 1): (0,), (1, 4): (0,), (2, 0): (0,), (2, 1): (1,), (2, 4): (1, 0), (2, 6): (0,)
     }
     enter_step(0)
     for place, (chunk, block) in enumerate(steps):
@@ -717,9 +732,10 @@
         advance(*after_block.get((chunk, block), ()))
     leave_step(len(steps) - 1)
     finish_chunk(CHUNKS - 1)
-    advance(2, 1)
+    advance(2)
+    advance(1)
     first = 0
-    for last, which in ((7, (2, 0)), (14, (0, 1))):
+    for last, which in ((5, (2,)), (10, (0,)), (14, (1,))):
         after_mlp(
             first, last, branch, grad_xn, cot_masked, padded, centred, inv_std, mask, scale, gain, mixed,
             grad_conv, sums,
@@ -727,15 +743,23 @@
         advance(*which)
         first = last
     store(mixed, mixed_out)
+    collect_vectors(sums, in_sums, small)
     first = 0
-    for last, which in ((7, (1,)), (12, (2,)), (16, (0,)), (20, (1,)), (26, (2,)), (30, (0, 2)), (35, (1, 2)), (39, ())):
+    for last, which in (
+        (5, (2,)), (10, (0, 1)), (16, (2,)), (22, (0, 1)), (27, (2,)), (33, (1,)), (39, ())
+    ):
         conv_grad(first, last, padded, grad_conv, tap_sums)
         advance(*which)
         first = last
-    collect(tap_sums, sums, in_sums, small)
+    collect_taps(tap_sums, small)
     advance(3)
+    for which in (2, 1, 3, 2, 3, 2, 3):
+        advance(which)
     while any(item.phase < item.phases for item in running):
-        advance(2, 3, 0, 1)
+        advance(2)
+        advance(3)
+        advance(1)
+        advance(0)
     for made in copies:
         made.wait()
     for made in halves:
@@ -863,7 +887,7 @@
     mixed, large, small = run_block(
         features[0],
         cotangent[0],
-        owner_slot[0],
+        owner_slot[0].T,
         dw_weight,
         dw_bias,
         ln_gain,

time: 120 us -> 108 us (0.900)
  Pallas kernels: 118 us -> 106 us
    pallas_call x1, Pallas kernels: 113 us -> 101 us  [run_block(): pl.pallas_call(block_kernel, out_shape=(jax.ShapeDtypeStruct((ROWS, BREAD...]
where the time goes in v4:
time: 108 us
  Pallas kernels  106 us (98%)
  local copies, waits for them, and re-layouts  1.29 us (1%)
    pallas_call x1, Pallas kernels, run_block(): pl.pallas_call(block_kernel, out_shape=(jax.ShapeDtypeStruct((ROWS, BREAD...  101 us
    pallas_call x1, Pallas kernels, finish(): pl.pallas_call(finish_kernel, out_shape=(jax.ShapeDtypeStruct(mixed.shape...  4.63 us

profile of v4, /device:TPU:1, one launch (start us, length us, event | category | flops | bytes accessed | tf_op | source)
XLA Modules:
  0.0 107.6 jit_solution(6680942057666031279)
XLA Ops:
  0.6 1.3 %copy.24 = s32[1,64,14]{1,2,0:T(8,128)} copy(s32[1,64,14]{1,0,2:T(1,128)} %param.14) | data formatting | bytes 7168
  1.9 100.9 %shard_map.195 = (bf16[14,98,384]{2,1,0:T(8,128)(2,1)}, bf16[3,2,1536,128]{3,2,1,0:T(8,128)(2,1)}, f32[256,128]{1,0:T(8,128)}) custom-call(bf16[14,98,384]{2,1,0:T(8,128)(2,1)} %bitcast.8, bf16[14,98,384]{2,1,0:T(8,128)(2,1)} %bitcast.9, s32[14,64]{1,0:T(8,128)} %bitcast.10, f32[7,7,384]{2,1,0:T(8,128)} %dw_weight.1, f32[384]{0:T(512)} %dw_bias.1, f32[384]{0:T(512)} %gain.1, ...), custom_call_target="tpu_custom_call" | custom-call | tf_op jit(solution)/shard_map/pallas_call | solution.py:776
  102.8 4.6 %shard_map.196 = (bf16[14,98,384]{2,1,0:T(8,128)(2,1)}, f32[7,7,384]{2,1,0:T(8,128)}, f32[384]{0:T(512)}, f32[384]{0:T(512)}, f32[384]{0:T(512)}, /*index=5*/f32...) custom-call(bf16[14,98,384]{2,1,0:T(8,128)(2,1)} %get-tuple-element.23.mixed_in, ...), custom_call_target="tpu_custom_call" | custom-call | tf_op jit(solution)/shard_map/pallas_call | solution.py:852

commit v5 on v4

--- a/solution.py
+++ b/solution.py
@@ -72,7 +72,7 @@
     barrier = pltpu.get_barrier_semaphore()
     for peer in peers:
         pl.semaphore_signal(barrier, inc=1, device_id=peer, device_id_type=MESH)
-    pl.semaphore_wait(barrier, len(peers))
+    return barrier, len(peers)
 
 
 class Sum:
@@ -83,7 +83,6 @@
         for axis in scatter:
             self.heights.append(self.heights[-1] // SIZES[axis])
         self.phases = 2 * len(scatter) + len(exchange) + 3
-        self.copies = 2 + 2 * sum(SIZES[a] - 1 for a in scatter) + sum(SIZES[a] - 1 for a in exchange)
 
     def scratch(self):
         shapes = [pltpu.VMEM((self.rows, LANES), jnp.float32)]
@@ -93,8 +92,8 @@
             shapes.append(pltpu.VMEM((SIZES[axis] - 1, after, LANES), self.dtype))
         for axis in self.exchange:
             shapes.append(pltpu.VMEM((SIZES[axis], self.heights[-1], LANES), self.dtype))
-        shapes.append(pltpu.SemaphoreType.DMA((self.copies,)))
-        shapes.append(pltpu.SemaphoreType.DMA((self.copies,)))
+        shapes.append(pltpu.SemaphoreType.DMA((self.phases,)))
+        shapes.append(pltpu.SemaphoreType.DMA((self.phases,)))
         return shapes
 
     def bind(self, where, keep, send, result, refs):
@@ -104,7 +103,6 @@
         self.levels = [tuple(refs.pop(0) for _ in range(3)) for _ in self.scatter]
         self.slots = [refs.pop(0) for _ in self.exchange]
         self.send_sems, self.recv_sems = refs
-        self.used = 0
         self.flying = []
         self.done = []
         self.phase = 0
@@ -115,18 +113,21 @@
             self.offsets.append(offset)
         return self
 
-    def copy(self, source, target, device):
+    def copy(self, source, target, device, start=True):
         made = pltpu.make_async_remote_copy(
             src_ref=source,
             dst_ref=target,
-            send_sem=self.send_sems.at[self.used],
-            recv_sem=self.recv_sems.at[self.used],
+            send_sem=self.send_sems.at[self.phase],
+            recv_sem=self.recv_sems.at[self.phase],
             device_id=device,
             device_id_type=MESH,
         )
-        self.used += 1
-        made.start()
-        self.flying.append(made)
+        if start:
+            made.start()
+        return made
+
+    def fly(self, everything, device):
+        self.flying.append(self.copy(everything, everything, device, start=False))
 
     def land(self):
         for made in self.flying:
@@ -140,6 +141,7 @@
     def start_core(self):
         other = device_at({**self.where, "core": 1 - self.where["core"]})
         self.copy(self.send, self.landed, other)
+        self.fly(self.landed, other)
 
     def start_scatter(self, index, total):
         axis, height = self.scatter[index], self.heights[index + 1]
@@ -153,6 +155,7 @@
                 incoming.at[step - 1],
                 device,
             )
+        self.fly(incoming, device)
 
     def finish_scatter(self, index):
         axis, height = self.scatter[index], self.heights[index + 1]
@@ -169,6 +172,7 @@
         for step in range(1, SIZES[axis]):
             _, device = peer_along(self.where, axis, step)
             self.copy(slots.at[me], slots.at[me], device)
+        self.fly(slots.at[pl.ds(0, SIZES[axis] - 1)], device)
 
     def finish_exchange(self, index):
         axis, slots = self.exchange[index], self.slots[index]
@@ -183,14 +187,20 @@
         for step in range(1, SIZES[axis]):
             _, device = peer_along(self.where, axis, step)
             self.copy(block, block, device)
+        count = (SIZES[axis] - 1) * self.heights[index + 1]
+        self.fly(self.result.at[core, pl.ds(0, count), :], device)
 
     def advance(self):
         phase, core = self.phase, self.where["core"]
         deep, wide = len(self.scatter), len(self.exchange)
         if phase >= self.phases:
             return False
+        self.land()
+        more = self.step(phase, deep, wide, core)
         self.phase += 1
-        self.land()
+        return more
+
+    def step(self, phase, deep, wide, core):
         if phase == 0:
             self.start_core()
             return True
@@ -217,6 +227,7 @@
         if step == deep:
             other = device_at({**self.where, "core": 1 - core})
             self.copy(self.result.at[core], self.result.at[core], other)
+            self.fly(self.result.at[core], other)
             return True
         for made in self.done:
             made.wait_send()
@@ -231,26 +242,31 @@
         return [
             pltpu.VMEM((15, self.ROWS, LANES), jnp.float32),
             pltpu.VMEM((16, self.ROWS, LANES), jnp.float32),
-            pltpu.SemaphoreType.DMA((45,)),
-            pltpu.SemaphoreType.DMA((45,)),
+            pltpu.SemaphoreType.DMA((3,)),
+            pltpu.SemaphoreType.DMA((3,)),
         ]
 
     def bind(self, where, source, result, refs):
         self.where, self.source, self.result = where, source, result
         self.landed, self.slots, self.send_sems, self.recv_sems = refs
-        self.used, self.phase = 0, 0
+        self.phase = 0
         self.flying, self.done = [], []
         return self
 
     copy = Sum.copy
+    fly = Sum.fly
     land = Sum.land
 
     def advance(self):
         phase, where, rows = self.phase, self.where, self.ROWS
         if phase >= self.phases:
             return False
+        self.land()
+        more = self.step(phase, where, rows)
         self.phase += 1
-        self.land()
+        return more
+
+    def step(self, phase, where, rows):
         place, flat = where["z"] * 2 + where["core"], where["y"] * 4 + where["x"]
         mine = pl.ds(pl.multiple_of(place * rows, rows), rows)
         if phase == 0:
@@ -258,6 +274,7 @@
                 other, device = stack_peer(where, step)
                 block = self.source.at[pl.ds(pl.multiple_of(other * rows, rows), rows), :]
                 self.copy(block, self.landed.at[step - 1], device)
+            self.fly(self.landed, device)
         elif phase == 1:
             total = self.source[mine, :]
             for step in range(15):
@@ -266,6 +283,7 @@
             for step in range(1, 16):
                 _, device = plane_peer(where, step)
                 self.copy(self.slots.at[flat], self.slots.at[flat], device)
+            self.fly(self.slots.at[pl.ds(0, 15)], device)
         elif phase == 2:
             total = self.slots[0]
             for index in range(1, 16):
@@ -275,6 +293,7 @@
             for step in range(1, 16):
                 _, device = stack_peer(where, step)
                 self.copy(block, block, device)
+            self.fly(self.result.at[pl.ds(0, 15 * rows), :], device)
         else:
             for made in self.done:
                 made.wait_send()
@@ -315,7 +334,7 @@
         if place == 3:
             inside = jnp.where(tile < 31, 1.0, 0.0)
         for column in range(COLS):
-            live = jnp.where(table[column, row] >= 0, 1.0, 0.0) * inside
+            live = jnp.where(table[column, 0, row] >= 0, 1.0, 0.0) * inside
             mask[place, column * TP : (column + 1) * TP, :] = jnp.full((TP, LANES), live, jnp.float32)
 
 
@@ -548,14 +567,7 @@
 
 
 X_FIRST, Y_FIRST = (("x", "z"), ("y",)), (("y", "z"), ("x",))
-PIECES = (
-    (0, 0, 1024, X_FIRST),
-    (0, 1024, 512, Y_FIRST),
-    (1, 0, 1024, Y_FIRST),
-    (1, 1024, 512, X_FIRST),
-    (2, 0, 1024, X_FIRST),
-    (2, 1024, 512, Y_FIRST),
-)
+PIECES = ((0, 0, 1536, X_FIRST), (1, 0, 1536, Y_FIRST), (2, 0, 1536, X_FIRST))
 
 
 def plan():
@@ -628,7 +640,10 @@
     ]
     for made in loads:
         made.start()
-    enter(where)
+    greeting = enter(where)
+    spread_tissue(table, mask)
+    spread_taps(dw_weight, taps, dw_bias, bias_rows)
+    pl.semaphore_wait(*greeting)
     halves = []
     for side, step, first in ((0, 1, ROWS - REACH), (1, 31, 0)):
         made = pltpu.make_async_remote_copy(
@@ -673,8 +688,6 @@
                 else:
                     store(small_held, small_out)
 
-    spread_tissue(table, mask)
-    spread_taps(dw_weight, taps, dw_bias, bias_rows)
     sums[...] = jnp.zeros(sums.shape, jnp.float32)
     tap_sums[...] = jnp.zeros(tap_sums.shape, jnp.float32)
     in_sums[...] = jnp.zeros(in_sums.shape, jnp.float32)
@@ -887,7 +900,7 @@
     mixed, large, small = run_block(
         features[0],
         cotangent[0],
-        owner_slot[0].T,
+        owner_slot.transpose(2, 0, 1),
         dw_weight,
         dw_bias,
         ln_gain,

time: 108 us -> 110 us (1.019)
  Pallas kernels: 106 us -> 109 us
  local copies, waits for them, and re-layouts: 1.29 us -> 0 us
    pallas_call x1, Pallas kernels: 101 us -> 104 us  [run_block(): pl.pallas_call(block_kernel, out_shape=(jax.ShapeDtypeStruct((ROWS, BREAD...]
    unnamed x1 -> x0, local copies, waits for them, and re-layouts: 1.29 us -> none
where the time goes in v5:
time: 110 us
  Pallas kernels  109 us (99%)
    pallas_call x1, Pallas kernels, run_block(): pl.pallas_call(block_kernel, out_shape=(jax.ShapeDtypeStruct((ROWS, BREAD...  104 us
    pallas_call x1, Pallas kernels, finish(): pl.pallas_call(finish_kernel, out_shape=(jax.ShapeDtypeStruct(mixed.shape...  4.63 us

profile of v5, /device:TPU:1, one launch (start us, length us, event | category | flops | bytes accessed | tf_op | source)
XLA Modules:
  0.0 109.5 jit_solution(6600581200012186124)
XLA Ops:
  0.6 104.1 %shard_map.195 = (bf16[14,98,384]{2,1,0:T(8,128)(2,1)}, bf16[3,2,1536,128]{3,2,1,0:T(8,128)(2,1)}, f32[256,128]{1,0:T(8,128)}) custom-call(bf16[14,98,384]{2,1,0:T(8,128)(2,1)} %bitcast.4, bf16[14,98,384]{2,1,0:T(8,128)(2,1)} %bitcast.5, s32[14,1,64]{2,1,0:T(1,128)} %bitcast.6, f32[7,7,384]{2,1,0:T(8,128)} %dw_weight.1, f32[384]{0:T(512)} %dw_bias.1, ...), custom_call_target="tpu_custom_call" | custom-call | tf_op jit(solution)/shard_map/pallas_call | solution.py:789
  104.7 4.6 %shard_map.196 = (bf16[14,98,384]{2,1,0:T(8,128)(2,1)}, f32[7,7,384]{2,1,0:T(8,128)}, f32[384]{0:T(512)}, f32[384]{0:T(512)}, f32[384]{0:T(512)}, /*index=5*/f32...) custom-call(bf16[14,98,384]{2,1,0:T(8,128)(2,1)} %get-tuple-element.23.mixed_in, ...), custom_call_target="tpu_custom_call" | custom-call | tf_op jit(solution)/shard_map/pallas_call | solution.py:865

commit v6 on v5

--- a/solution.py
+++ b/solution.py
@@ -397,22 +397,26 @@
 
 
 def conv_grad(first, last, padded, grad_conv, tap_sums):
-    def tile(step, carry):
-        group, column = step // 13, step % 13
-        pull = jnp.stack(
-            [
-                grad_conv[group, pl.ds(pl.multiple_of(i * WIDE + 8 * column, 8), 8), :]
-                for i in range(ROWS)
-            ]
-        )
-        for col_tap in range(K):
+    def unit(step, carry):
+        group, col_tap = step // K, step % K
+        totals = [jnp.zeros((8, LANES), jnp.float32)] * K
+        for column in range(13):
+            pull = jnp.stack(
+                [
+                    grad_conv[group, i * WIDE + 8 * column : i * WIDE + 8 * column + 8, :]
+                    for i in range(ROWS)
+                ]
+            )
             window = padded[group, :, pl.ds(8 * column + 5 + col_tap, 8), :]
             for row_tap in range(K):
-                tap = row_tap * K + col_tap
-                tap_sums[group, tap] += jnp.sum(window[row_tap : row_tap + ROWS] * pull, axis=0)
+                totals[row_tap] = totals[row_tap] + jnp.sum(
+                    window[row_tap : row_tap + ROWS] * pull, axis=0
+                )
+        for row_tap in range(K):
+            tap_sums[group, row_tap * K + col_tap] = totals[row_tap]
         return carry
 
-    lax.fori_loop(first, last, tile, 0)
+    lax.fori_loop(first, last, unit, 0)
 
 
 def norm(conv_out, inv_std, gain, offset, normed):
@@ -512,22 +516,24 @@
 
 
 def after_mlp(first, last, branch, grad_xn, cot_masked, padded, centred, inv_std, mask, scale, gain, mixed, grad_conv, sums):
-    def part(i, start, size):
+    def part(i, start, size, totals):
+        totals = list(totals)
         place = pl.ds(pl.multiple_of(i * WIDE + start, 8), size)
         live = mask[1 + i // TP, start : start + size]
         used = min(BREADTH - start, size)
-        pulls, held = [], []
+        kept = []
         for group in range(GROUPS):
             out = branch[place, lanes(group)].astype(jnp.bfloat16).astype(jnp.float32)
-            sums[3 + group] += by_eight(cot_masked[group, place, :] * out)
-            kept = padded[group, i + REACH, 8 + start : 8 + start + size, :]
-            kept = kept + live * (line(scale, group) * out)
-            mixed[i, start : start + used, lanes(group)] = kept[:used].astype(jnp.bfloat16)
+            totals[group] = totals[group] + by_eight(cot_masked[group, place, :] * out)
+            cells = padded[group, i + REACH, 8 + start : 8 + start + size, :]
+            cells = cells + live * (line(scale, group) * out)
+            kept.append(cells[:used].astype(jnp.bfloat16))
+        pulls, held = [], []
         for group in range(GROUPS):
             pull = grad_xn[place, lanes(group)].astype(jnp.bfloat16).astype(jnp.float32)
             cen = centred[group, place, :]
-            sums[6 + group] += by_eight(pull * cen)
-            sums[9 + group] += by_eight(pull)
+            totals[3 + group] = totals[3 + group] + by_eight(pull * cen)
+            totals[6 + group] = totals[6 + group] + by_eight(pull)
             pulls.append(pull * line(gain, group))
             held.append(cen)
         mean = jnp.sum(pulls[0] + pulls[1] + pulls[2], axis=-1, keepdims=True) * (1.0 / C)
@@ -535,16 +541,19 @@
         along = jnp.sum(along, axis=-1, keepdims=True) * (1.0 / C)
         inv = inv_std[place, :]
         for group in range(GROUPS):
-            pull = inv * (pulls[group] - mean - held[group] * along)
-            grad_conv[group, place, :] = pull
-            sums[12 + group] += by_eight(pull)
-
-    def row(i, carry):
-        part(i, 0, 48)
-        part(i, 48, 56)
-        return carry
-
-    lax.fori_loop(first, last, row, 0)
+            pulls[group] = inv * (pulls[group] - mean - held[group] * along)
+            totals[9 + group] = totals[9 + group] + by_eight(pulls[group])
+        for group in range(GROUPS):
+            mixed[i, start : start + used, lanes(group)] = kept[group]
+            grad_conv[group, place, :] = pulls[group]
+        return tuple(totals)
+
+    def row(i, totals):
+        return part(i, 48, 56, part(i, 0, 48, totals))
+
+    totals = lax.fori_loop(first, last, row, tuple(sums[3 + index] for index in range(12)))
+    for index in range(12):
+        sums[3 + index] = totals[index]
 
 
 def put(small, place, value):
@@ -567,7 +576,14 @@
 
 
 X_FIRST, Y_FIRST = (("x", "z"), ("y",)), (("y", "z"), ("x",))
-PIECES = ((0, 0, 1536, X_FIRST), (1, 0, 1536, Y_FIRST), (2, 0, 1536, X_FIRST))
+PIECES = (
+    (0, 0, 1024, X_FIRST),
+    (0, 1024, 512, Y_FIRST),
+    (1, 0, 1024, Y_FIRST),
+    (1, 1024, 512, X_FIRST),
+    (2, 0, 1024, X_FIRST),
+    (2, 1024, 512, Y_FIRST),
+)
 
 
 def plan():
@@ -689,7 +705,6 @@
                     store(small_held, small_out)
 
     sums[...] = jnp.zeros(sums.shape, jnp.float32)
-    tap_sums[...] = jnp.zeros(tap_sums.shape, jnp.float32)
     in_sums[...] = jnp.zeros(in_sums.shape, jnp.float32)
     for rows in (normed, grad_branch, hidden.at[0], hidden.at[1], grad_pre.at[0], grad_pre.at[1]):
         rows[CELLS:, :] = jnp.zeros((PADDED - CELLS, rows.shape[1]), jnp.bfloat16)
@@ -727,9 +742,7 @@
         half = chunk % 2
         weight_grads(chunk, normed_t, grad_branch_t, hidden.at[half], grad_pre.at[half], large)
 
-    after_block = {
-        (1, 1): (0,), (1, 4): (0,), (2, 0): (0,), (2, 1): (1,), (2, 4): (1, 0), (2, 6): (0,)
-    }
+    after_block = {(1, 0): (0,), (1, 4): (0,), (2, 0): (1,), (2, 3): (0,), (2, 4): (1,)}
     enter_step(0)
     for place, (chunk, block) in enumerate(steps):
         half, side = chunk % 2, place % 2
@@ -746,28 +759,27 @@
     leave_step(len(steps) - 1)
     finish_chunk(CHUNKS - 1)
     advance(2)
-    advance(1)
+    advance(0)
     first = 0
-    for last, which in ((5, (2,)), (10, (0,)), (14, (1,))):
+    for last, which in ((8, (0,)), (14, (2, 1))):
         after_mlp(
             first, last, branch, grad_xn, cot_masked, padded, centred, inv_std, mask, scale, gain, mixed,
             grad_conv, sums,
         )
-        advance(*which)
+        for chunk in which:
+            advance(chunk)
         first = last
     store(mixed, mixed_out)
     collect_vectors(sums, in_sums, small)
     first = 0
-    for last, which in (
-        (5, (2,)), (10, (0, 1)), (16, (2,)), (22, (0, 1)), (27, (2,)), (33, (1,)), (39, ())
-    ):
+    for last, which in ((7, (0,)), (14, (2, 1)), (21, (2,))):
         conv_grad(first, last, padded, grad_conv, tap_sums)
-        advance(*which)
+        for chunk in which:
+            advance(chunk)
         first = last
     collect_taps(tap_sums, small)
-    advance(3)
-    for which in (2, 1, 3, 2, 3, 2, 3):
-        advance(which)
+    for chunk in (3, 2, 1, 3, 0, 2, 1, 3, 1, 2, 3):
+        advance(chunk)
     while any(item.phase < item.phases for item in running):
         advance(2)
         advance(3)

time: 110 us -> 99.7 us (0.906)
  Pallas kernels: 109 us -> 98.7 us
    pallas_call x1, Pallas kernels: 104 us -> 94.1 us  [run_block(): pl.pallas_call(block_kernel, out_shape=(jax.ShapeDtypeStruct((ROWS, BREAD...]
where the time goes in v6:
time: 99.7 us; the launch traced here: 99.5 us
  Pallas kernels  98.7 us (99%)
    pallas_call x1, Pallas kernels, run_block(): pl.pallas_call(block_kernel, out_shape=(jax.ShapeDtypeStruct((ROWS, BREAD...  94.1 us
    pallas_call x1, Pallas kernels, finish(): pl.pallas_call(finish_kernel, out_shape=(jax.ShapeDtypeStruct(mixed.shape...  4.63 us

profile of v6, /device:TPU:1, one launch (start us, length us, event | category | flops | bytes accessed | tf_op | source)
XLA Modules:
  0.0 99.5 jit_solution(5667545882739129442)
XLA Ops:
  0.6 94.1 %shard_map.195 = (bf16[14,98,384]{2,1,0:T(8,128)(2,1)}, bf16[3,2,1536,128]{3,2,1,0:T(8,128)(2,1)}, f32[256,128]{1,0:T(8,128)}) custom-call(bf16[14,98,384]{2,1,0:T(8,128)(2,1)} %bitcast.4, bf16[14,98,384]{2,1,0:T(8,128)(2,1)} %bitcast.5, s32[14,1,64]{2,1,0:T(1,128)} %bitcast.6, f32[7,7,384]{2,1,0:T(8,128)} %dw_weight.1, f32[384]{0:T(512)} %dw_bias.1, ...), custom_call_target="tpu_custom_call" | custom-call | tf_op jit(solution)/shard_map/pallas_call | solution.py:801
  94.8 4.6 %shard_map.196 = (bf16[14,98,384]{2,1,0:T(8,128)(2,1)}, f32[7,7,384]{2,1,0:T(8,128)}, f32[384]{0:T(512)}, f32[384]{0:T(512)}, f32[384]{0:T(512)}, /*index=5*/f32...) custom-call(bf16[14,98,384]{2,1,0:T(8,128)(2,1)} %get-tuple-element.23.mixed_in, ...), custom_call_target="tpu_custom_call" | custom-call | tf_op jit(solution)/shard_map/pallas_call | solution.py:877

commit v7 on v6

--- a/solution.py
+++ b/solution.py
@@ -452,13 +452,9 @@
     lax.fori_loop(0, CELLS // NORM_ROWS, block, 0)
 
 
-def turn(rows, turned):
-    def block(step, carry):
-        place = pl.ds(pl.multiple_of(step * LANES, LANES), LANES)
-        turned[:, place] = rows[place, :].T
-        return carry
-
-    lax.fori_loop(0, PADDED // LANES, block, 0)
+def turn(index, rows, turned):
+    place = slice(index * LANES, (index + 1) * LANES)
+    turned[:, place] = rows[place, :].T
 
 
 def nt(left, right):
@@ -576,13 +572,15 @@
 
 
 X_FIRST, Y_FIRST = (("x", "z"), ("y",)), (("y", "z"), ("x",))
+Z_FIRST = (("z", "y"), ("x",))
 PIECES = (
     (0, 0, 1024, X_FIRST),
     (0, 1024, 512, Y_FIRST),
     (1, 0, 1024, Y_FIRST),
     (1, 1024, 512, X_FIRST),
-    (2, 0, 1024, X_FIRST),
-    (2, 1024, 512, Y_FIRST),
+    (2, 0, 512, X_FIRST),
+    (2, 512, 512, Y_FIRST),
+    (2, 1024, 512, Z_FIRST),
 )
 
 
@@ -711,13 +709,11 @@
     loads[0].wait()
     fill(feat, cot, mask, padded, cot_masked)
     branch_grad(cot_masked, scale, grad_branch, sums)
-    turn(grad_branch, grad_branch_t)
     for made in halves:
         made.wait_recv()
     fill_halo(halo, mask, padded)
     conv(padded, taps, bias_rows, centred)
     norm(centred, inv_std, gain, offset, normed)
-    turn(normed, normed_t)
     loads[1].wait()
     loads[2].wait()
 
@@ -751,6 +747,10 @@
             chunk, block, b_in, pre_act.at[side], pull.at[side], hidden.at[half], grad_pre.at[half],
             in_sums,
         )
+        if place < 6:
+            for index in (2 * place, 2 * place + 1):
+                turn(index, normed, normed_t)
+                turn(index, grad_branch, grad_branch_t)
         if place > 0:
             leave_step(place - 1)
         if block == 0 and chunk > 0:
@@ -761,7 +761,7 @@
     advance(2)
     advance(0)
     first = 0
-    for last, which in ((8, (0,)), (14, (2, 1))):
+    for last, which in ((8, (0,)), (11, (2,)), (14, (1,))):
         after_mlp(
             first, last, branch, grad_xn, cot_masked, padded, centred, inv_std, mask, scale, gain, mixed,
             grad_conv, sums,
@@ -772,13 +772,13 @@
     store(mixed, mixed_out)
     collect_vectors(sums, in_sums, small)
     first = 0
-    for last, which in ((7, (0,)), (14, (2, 1)), (21, (2,))):
+    for last, which in ((5, (0,)), (10, (2, 1)), (16, (2,)), (21, (2,))):
         conv_grad(first, last, padded, grad_conv, tap_sums)
         for chunk in which:
             advance(chunk)
         first = last
     collect_taps(tap_sums, small)
-    for chunk in (3, 2, 1, 3, 0, 2, 1, 3, 1, 2, 3):
+    for chunk in (3, 1, 0, 3, 2, 3, 1, 2, 3, 1, 2):
         advance(chunk)
     while any(item.phase < item.phases for item in running):
         advance(2)

time: 99.7 us -> 101 us (1.013)
  Pallas kernels: 98.7 us -> 100 us
    pallas_call x1, Pallas kernels: 94.1 us -> 95.5 us  [run_block(): pl.pallas_call(block_kernel, out_shape=(jax.ShapeDtypeStruct((ROWS, BREAD...]
where the time goes in v7:
time: 101 us
  Pallas kernels  100 us (99%)
    pallas_call x1, Pallas kernels, run_block(): pl.pallas_call(block_kernel, out_shape=(jax.ShapeDtypeStruct((ROWS, BREAD...  95.5 us
    pallas_call x1, Pallas kernels, finish(): pl.pallas_call(finish_kernel, out_shape=(jax.ShapeDtypeStruct(mixed.shape...  4.63 us

profile of v7, /device:TPU:1, one launch (start us, length us, event | category | flops | bytes accessed | tf_op | source)
XLA Modules:
  0.0 100.9 jit_solution(430788487224396206)
XLA Ops:
  0.6 95.5 %shard_map.195 = (bf16[14,98,384]{2,1,0:T(8,128)(2,1)}, bf16[3,2,1536,128]{3,2,1,0:T(8,128)(2,1)}, f32[256,128]{1,0:T(8,128)}) custom-call(bf16[14,98,384]{2,1,0:T(8,128)(2,1)} %bitcast.4, bf16[14,98,384]{2,1,0:T(8,128)(2,1)} %bitcast.5, s32[14,1,64]{2,1,0:T(1,128)} %bitcast.6, f32[7,7,384]{2,1,0:T(8,128)} %dw_weight.1, f32[384]{0:T(512)} %dw_bias.1, ...), custom_call_target="tpu_custom_call" | custom-call | tf_op jit(solution)/shard_map/pallas_call | solution.py:801
  96.1 4.6 %shard_map.196 = (bf16[14,98,384]{2,1,0:T(8,128)(2,1)}, f32[7,7,384]{2,1,0:T(8,128)}, f32[384]{0:T(512)}, f32[384]{0:T(512)}, f32[384]{0:T(512)}, /*index=5*/f32...) custom-call(bf16[14,98,384]{2,1,0:T(8,128)(2,1)} %get-tuple-element.23.mixed_in, ...), custom_call_target="tpu_custom_call" | custom-call | tf_op jit(solution)/shard_map/pallas_call | solution.py:877

commit v8 on v6

--- a/solution.py
+++ b/solution.py
@@ -382,18 +382,19 @@
 
 
 def conv(padded, taps, bias_rows, conv_out):
-    def tile(step, carry):
-        group, column = step // 13, step % 13
-        total = jnp.zeros((ROWS, 8, LANES), jnp.float32) + bias_rows[group]
-        for col_tap in range(K):
-            window = padded[group, :, pl.ds(8 * column + 5 + col_tap, 8), :]
-            for row_tap in range(K):
-                total = total + window[row_tap : row_tap + ROWS] * taps[group, row_tap * K + col_tap]
-        for i in range(ROWS):
-            conv_out[group, pl.ds(pl.multiple_of(i * WIDE + 8 * column, 8), 8), :] = total[i]
+    def one(group, carry):
+        for column in range(13):
+            total = jnp.zeros((ROWS, 8, LANES), jnp.float32) + bias_rows[group]
+            for col_tap in range(K):
+                window = padded[group, :, 8 * column + 5 + col_tap : 8 * column + 13 + col_tap, :]
+                for row_tap in range(K):
+                    tap = row_tap * K + col_tap
+                    total = total + window[row_tap : row_tap + ROWS] * taps[group, tap]
+            for i in range(ROWS):
+                conv_out[group, i * WIDE + 8 * column : i * WIDE + 8 * column + 8, :] = total[i]
         return carry
 
-    lax.fori_loop(0, GROUPS * 13, tile, 0)
+    lax.fori_loop(0, GROUPS, one, 0)
 
 
 def conv_grad(first, last, padded, grad_conv, tap_sums):
@@ -828,20 +829,6 @@
     ]
     for made in [little, arrive] + loads:
         made.start()
-    little.wait()
-
-    def row(place):
-        return small[place : place + 1, :]
-
-    for group in range(GROUPS):
-        for tap in range(K * K):
-            dw[tap // K, tap % K : tap % K + 1, lanes(group)] = row(group * K * K + tap)
-    for index, target in enumerate((b2, scale, ln_gain, ln_bias, dwb)):
-        for group in range(GROUPS):
-            target[lanes(group)] = row(147 + index * GROUPS + group).reshape(LANES)
-    for group in range(HID // LANES):
-        b1[lanes(group)] = row(162 + group).reshape(LANES)
-
     arrive.wait()
     leave.start()
     stores = []
@@ -863,6 +850,19 @@
             made = pltpu.make_async_copy(w2.at[units, :], w2_out.at[units, :], out_sems.at[index])
         made.start()
         stores.append(made)
+    little.wait()
+
+    def row(place):
+        return small[place : place + 1, :]
+
+    for group in range(GROUPS):
+        for tap in range(K * K):
+            dw[tap // K, tap % K : tap % K + 1, lanes(group)] = row(group * K * K + tap)
+    for index, target in enumerate((b2, scale, ln_gain, ln_bias, dwb)):
+        for group in range(GROUPS):
+            target[lanes(group)] = row(147 + index * GROUPS + group).reshape(LANES)
+    for group in range(HID // LANES):
+        b1[lanes(group)] = row(162 + group).reshape(LANES)
     for made in stores + [leave]:
         made.wait()
 

time: 99.7 us -> 99.4 us (level)
  no operation moved by 1% of the time
where the time goes in v8:
time: 99.4 us; the launch traced here: 99.3 us
  Pallas kernels  98.5 us (99%)
    pallas_call x1, Pallas kernels, run_block(): pl.pallas_call(block_kernel, out_shape=(jax.ShapeDtypeStruct((ROWS, BREAD...  93.8 us
    pallas_call x1, Pallas kernels, finish(): pl.pallas_call(finish_kernel, out_shape=(jax.ShapeDtypeStruct(mixed.shape...  4.63 us

profile of v8, /device:TPU:1, one launch (start us, length us, event | category | flops | bytes accessed | tf_op | source)
XLA Modules:
  0.0 99.3 jit_solution(14829185041711141102)
XLA Ops:
  0.6 93.8 %shard_map.195 = (bf16[14,98,384]{2,1,0:T(8,128)(2,1)}, bf16[3,2,1536,128]{3,2,1,0:T(8,128)(2,1)}, f32[256,128]{1,0:T(8,128)}) custom-call(bf16[14,98,384]{2,1,0:T(8,128)(2,1)} %bitcast.4, bf16[14,98,384]{2,1,0:T(8,128)(2,1)} %bitcast.5, s32[14,1,64]{2,1,0:T(1,128)} %bitcast.6, f32[7,7,384]{2,1,0:T(8,128)} %dw_weight.1, f32[384]{0:T(512)} %dw_bias.1, ...), custom_call_target="tpu_custom_call" | custom-call | tf_op jit(solution)/shard_map/pallas_call | solution.py:802
  94.5 4.6 %shard_map.196 = (bf16[14,98,384]{2,1,0:T(8,128)(2,1)}, f32[7,7,384]{2,1,0:T(8,128)}, f32[384]{0:T(512)}, f32[384]{0:T(512)}, f32[384]{0:T(512)}, /*index=5*/f32...) custom-call(bf16[14,98,384]{2,1,0:T(8,128)(2,1)} %get-tuple-element.23.mixed_in, ...), custom_call_target="tpu_custom_call" | custom-call | tf_op jit(solution)/shard_map/pallas_call | solution.py:877
